TPU v7x, 256 devices: a whole 4x4x8 slice. The times are simulated.
256 devices in a mesh: dp: 2 (over x_hi), mp: 128 (over y, x_lo, z, core).
Axes of the slice: x: 4 (x_hi: 2, x_lo: 2; x = x_hi * 2 + x_lo), y: 4, z: 8, core: 2. Of those that a mesh axis runs over, the one named last changes fastest.
Arguments:
- activations: bfloat16 [2048, 16384], P('dp', 'mp'), may hold values from -6 to 6
- left_up: bfloat16 [128, 128, 128], P('mp'), may hold values from -0.5 to 0.5
- right_up: bfloat16 [128, 128, 128], P('mp'), may hold values from -0.5 to 0.5
- left_down: bfloat16 [128, 128, 128], P('mp'), may hold values from -0.5 to 0.5
- right_down: bfloat16 [128, 128, 128], P('mp'), may hold values from -0.5 to 0.5
- cotangent: bfloat16 [2048, 16384], P('dp', 'mp'), may hold values from -6 to 6
Outputs:
- mlp_output: bfloat16 [2048, 16384], P('dp', 'mp')
- input_grad: bfloat16 [2048, 16384], P('dp', 'mp')
- leftup_grad: float32 [128, 128, 128], P('mp')
- rightup_grad: float32 [128, 128, 128], P('mp')
- leftdown_grad: float32 [128, 128, 128], P('mp')
- rightdown_grad: float32 [128, 128, 128], P('mp')
All inputs are finite; a program needn't handle non-finite values.
Results may differ from a plain program's by a relative error of at most 0.011.
Values may be sent and summed in bfloat16 or wider, within the bound.
No kernel may reach another device: no remote copies, remote signals or barrier semaphores. Data moves between devices by JAX's collectives and lax.ppermute only.
A program may use at most 64 MiB of HBM per device.

v0:
```python
import math

import jax
import jax.numpy as jnp
from jax import lax
from jax.sharding import PartitionSpec as P


def gelu_exact(value):
    return 0.5 * value * (1.0 + lax.erf(value / math.sqrt(2.0)))


def gelu_slope(value):
    cumul = 0.5 * (1.0 + lax.erf(value / math.sqrt(2.0)))
    density = jnp.exp(-0.5 * value * value) / math.sqrt(2.0 * math.pi)
    return cumul + value * density


def left_blocks(vector, left):
    count = vector.shape[0]
    shaped = vector.reshape(count, left.shape[0], left.shape[1])
    return jnp.einsum("tbi,bij->tbj", shaped, left, preferred_element_type=jnp.float32).astype(
        jnp.bfloat16
    )


def monarch_forward(vector, left, right):
    blocks = left_blocks(vector, left)
    piece = lax.all_to_all(blocks, "mp", split_axis=2, concat_axis=1, tiled=True)
    result = jnp.einsum("tbj,jbk->tjk", piece, right, preferred_element_type=jnp.float32)
    return (piece, result)


def replayed(vector, left):
    blocks = left_blocks(vector, left)
    return lax.all_to_all(blocks, "mp", split_axis=2, concat_axis=1, tiled=True)


def monarch_backward(grad_out, permuted, right, left):
    back_perm = jnp.einsum(
        "tjk,jbk->tbj", grad_out, right, preferred_element_type=jnp.float32
    ).astype(jnp.bfloat16)
    piece = lax.all_to_all(back_perm, "mp", split_axis=1, concat_axis=2, tiled=True)
    input_back = jnp.einsum("tbj,bij->tbi", piece, left, preferred_element_type=jnp.float32)
    right_grad = jnp.einsum("tbj,tjk->jbk", permuted, grad_out, preferred_element_type=jnp.float32)
    return (input_back, piece, right_grad)


def pair_sum(left_grad, right_grad):
    return (
        lax.psum(left_grad.astype(jnp.bfloat16), "dp").astype(jnp.float32),
        lax.psum(right_grad.astype(jnp.bfloat16), "dp").astype(jnp.float32),
    )


def body(activations, left_up, right_up, left_down, right_down, cotangent):
    count = activations.shape[0]
    block_rows = left_up.shape[0]
    order = left_up.shape[1]
    first_perm, pre_act = monarch_forward(activations, left_up, right_up)
    hidden = gelu_exact(pre_act).astype(jnp.bfloat16).reshape(count, -1)
    second_perm, second_res = monarch_forward(hidden, left_down, right_down)
    mlp_output = second_res.astype(jnp.bfloat16).reshape(count, -1)
    gview = cotangent.reshape(count, -1, order)
    second_perm = replayed(hidden, left_down)
    hidden_back, second_back, grad_rd = monarch_backward(gview, second_perm, right_down, left_down)
    hview = hidden.reshape(count, block_rows, order)
    grad_ld = jnp.einsum("tbi,tbj->bij", hview, second_back, preferred_element_type=jnp.float32)
    grad_ld, grad_rd = pair_sum(grad_ld, grad_rd)
    pre_back = (hidden_back * gelu_slope(pre_act)).astype(jnp.bfloat16)
    first_perm = replayed(activations, left_up)
    input_back, first_back, grad_ru = monarch_backward(pre_back, first_perm, right_up, left_up)
    xview = activations.reshape(count, block_rows, order)
    grad_lu = jnp.einsum("tbi,tbj->bij", xview, first_back, preferred_element_type=jnp.float32)
    grad_lu, grad_ru = pair_sum(grad_lu, grad_ru)
    input_grad = input_back.astype(jnp.bfloat16).reshape(count, -1)
    return (mlp_output, input_grad, grad_lu, grad_ru, grad_ld, grad_rd)


def solution(mesh):
    placed = (
        P("dp", "mp"),
        P("mp", None, None),
        P("mp", None, None),
        P("mp", None, None),
        P("mp", None, None),
        P("dp", "mp"),
    )
    return jax.shard_map(
        body,
        mesh=mesh,
        in_specs=placed,
        out_specs=(
            P("dp", "mp"),
            P("dp", "mp"),
            P("mp", None, None),
            P("mp", None, None),
            P("mp", None, None),
            P("mp", None, None),
        ),
        check_vma=False,
    )
```

profile of v0, /device:TPU:1, one launch (start us, length us, event | category | flops | bytes accessed | tf_op | source)
XLA Modules:
  0.0 144.8 jit_solution(3145332724735700466)
XLA Ops:
  7.2 0.0 copy-start
  7.2 1.3 fusion.3
  8.4 0.4 copy.30
  8.9 0.5 broadcast.26
  9.4 2.1 %reduce = bf16[128,1024]{1,0:T(8,128)(2,1)S(1)} reduce(bf16[128,1,1024]{2,1,0:T(2,128)(2,1)S(1)} %bitcast.116, bf16[]{:T(256)} %broadcast.26), dimensions={1}, to_apply=%bitcast.111.reduce_sub_computation | reduce | bytes 524290
  11.5 0.9 reshape.118
  12.4 0.0 copy-start.3
  12.4 15.0 %all-to-all-start = ((bf16[128,2,512]{2,1,0:T(2,128)(2,1)}), bf16[128,2,512]{2,1,0:T(2,128)(2,1)S(1)}, u32[]{:S(2)}, u32[]{:S(2)}) async-start(bf16[128,2,512]{2,1,0:T(2,128)(2,1)} %reshape.118), calls=%async_computation | async-start | bytes 524288 | tf_op jit(solution)/shard_map/all_to_all | solution.py:29
  27.4 0.0 copy-done
  27.4 0.0 copy-done.3
  27.4 0.2 fusion.5
  27.7 0.4 copy.29
  28.1 2.2 %reduce.2 = bf16[128,1024]{1,0:T(8,128)(2,1)S(1)} reduce(bf16[128,1,1024]{2,1,0:T(2,128)(2,1)S(1)} %bitcast.118, bf16[]{:T(256)} %broadcast.26), dimensions={1}, to_apply=%bitcast.110.reduce_sub_computation | reduce | bytes 524290
  30.2 0.9 reshape.120
  31.1 10.9 %all-to-all-done = bf16[128,2,512]{2,1,0:T(2,128)(2,1)S(1)} async-done(((bf16[128,2,512]{2,1,0:T(2,128)(2,1)}), bf16[128,2,512]{2,1,0:T(2,128)(2,1)S(1)}, u32[]{:S(2)}, u32[]{:S(2)}) %all-to-all-start) | async-done | bytes 262176 | tf_op jit(solution)/shard_map/all_to_all | solution.py:29
  42.1 5.5 %all-to-all-start.2 = ((bf16[128,2,512]{2,1,0:T(2,128)(2,1)}), bf16[128,2,512]{2,1,0:T(2,128)(2,1)S(1)}, u32[]{:S(2)}, u32[]{:S(2)}) async-start(bf16[128,2,512]{2,1,0:T(2,128)(2,1)} %reshape.120), calls=%async_computation.2 | async-start | bytes 524288 | tf_op jit(solution)/shard_map/all_to_all | solution.py:43
  47.6 0.2 reshape.119
  47.9 0.0 copy-start.2
  47.9 0.4 copy.19
  48.3 0.3 copy-done.2
  48.6 0.2 convolution_bitcast_fusion.1
  48.8 0.0 copy-start.5
  48.9 0.1 fusion.15
  49.0 0.6 copy-done.5
  49.6 0.2 fusion.4
  49.8 0.5 copy.20
  50.3 2.2 %reduce.1 = bf16[128,1024]{1,0:T(8,128)(2,1)S(1)} reduce(bf16[128,1,1024]{2,1,0:T(2,128)(2,1)S(1)} %bitcast.119, bf16[]{:T(256)} %broadcast.26), dimensions={1}, to_apply=%bitcast.98.reduce_sub_computation | reduce | bytes 524290
  52.5 0.9 reshape.124
  53.4 9.0 %all-to-all-done.2 = bf16[128,2,512]{2,1,0:T(2,128)(2,1)S(1)} async-done(((bf16[128,2,512]{2,1,0:T(2,128)(2,1)}), bf16[128,2,512]{2,1,0:T(2,128)(2,1)S(1)}, u32[]{:S(2)}, u32[]{:S(2)}) %all-to-all-start.2) | async-done | bytes 262176 | tf_op jit(solution)/shard_map/all_to_all | solution.py:43
  62.4 5.7 %all-to-all-start.1 = ((bf16[128,2,512]{2,1,0:T(2,128)(2,1)}), bf16[128,2,512]{2,1,0:T(2,128)(2,1)S(1)}, u32[]{:S(2)}, u32[]{:S(2)}) async-start(bf16[128,2,512]{2,1,0:T(2,128)(2,1)} %reshape.124), calls=%async_computation.1 | async-start | bytes 524288 | tf_op jit(solution)/shard_map/all_to_all | solution.py:29
  68.1 0.2 reshape.121
  68.4 0.4 copy.23
  68.8 0.3 fusion.2
  69.1 0.2 fusion.6
  69.4 0.5 copy.24
  69.9 2.2 %reduce.3 = bf16[128,1024]{1,0:T(8,128)(2,1)S(1)} reduce(bf16[128,1,1024]{2,1,0:T(2,128)(2,1)S(1)} %bitcast.117, bf16[]{:T(256)} %broadcast.26), dimensions={1}, to_apply=%bitcast.96.reduce_sub_computation | reduce | bytes 524290
  72.0 0.9 reshape.122
  72.9 10.0 %all-to-all-done.1 = bf16[128,2,512]{2,1,0:T(2,128)(2,1)S(1)} async-done(((bf16[128,2,512]{2,1,0:T(2,128)(2,1)}), bf16[128,2,512]{2,1,0:T(2,128)(2,1)S(1)}, u32[]{:S(2)}, u32[]{:S(2)}) %all-to-all-start.1) | async-done | bytes 262176 | tf_op jit(solution)/shard_map/all_to_all | solution.py:29
  82.9 5.5 %all-to-all-start.3 = ((bf16[128,2,512]{2,1,0:T(2,128)(2,1)}), bf16[128,2,512]{2,1,0:T(2,128)(2,1)S(1)}, u32[]{:S(2)}, u32[]{:S(2)}) async-start(bf16[128,2,512]{2,1,0:T(2,128)(2,1)} %reshape.122), calls=%async_computation.3 | async-start | bytes 524288 | tf_op jit(solution)/shard_map/all_to_all | solution.py:43
  88.4 0.0 all-reduce.3.cloned.1.call-start
  88.5 0.9 fusion.9
  89.4 0.9 fusion.8
  90.2 0.2 reshape.125
  90.5 0.4 copy.21
  90.9 0.9 fusion.10
  91.8 0.9 convolution_convert_fusion.3
  92.7 10.5 %all-to-all-done.3 = bf16[128,2,512]{2,1,0:T(2,128)(2,1)S(1)} async-done(((bf16[128,2,512]{2,1,0:T(2,128)(2,1)}), bf16[128,2,512]{2,1,0:T(2,128)(2,1)S(1)}, u32[]{:S(2)}, u32[]{:S(2)}) %all-to-all-start.3) | async-done | bytes 262176 | tf_op jit(solution)/shard_map/all_to_all | solution.py:43
  103.2 0.2 reshape.123
  103.4 0.0 copy-start.1
  103.4 0.4 copy.25
  103.9 0.5 copy-done.1
  104.4 0.9 fusion.7
  105.2 0.0 copy-start.4
  105.3 0.0 all-reduce.3.cloned.1.call-update
  105.3 0.7 copy-done.4
  106.0 0.9 convolution_convert_fusion
  106.9 27.4 %all-reduce.3.cloned.1.call-done = (bf16[1,128,128]{1,2,0:T(8,128)(2,1)}, bf16[1,128,128]{2,1,0:T(8,128)(2,1)}, bf16[1,128,128]{2,1,0:T(8,128)(2,1)}, bf16[1,128,128]{2,1,0:T(8,128)(2,1)}) async-done(((bf16[1,128,128]{1,2,0:T(8,128)(2,1)}, bf16[1,128,128]{2,1,0:T(8,128)(2,1)}, bf16[1,128,128]{2,1,0:T(8,128)(2,1)}, bf16[1,128,128]{2,1,0:T(8,128)(2,1)}), (bf16[1,128,128]{1,2,0:T(8,128)(2,1)}, ...) | async-done | bytes 131088 | tf_op jit(solution)/shard_map/psum | solution.py:51
  134.3 1.5 %copy.26 = f32[1,128,128]{2,1,0:T(8,128)} copy(bf16[1,128,128]{1,2,0:T(8,128)(2,1)} %get-tuple-element.24) | data formatting | bytes 98304
  135.8 0.0 copy-done.8
  135.8 0.6 convert_element_type.125
  136.4 0.1 copy-done.7
  136.6 0.6 convert_element_type.128
  137.2 0.1 copy-done.6
  137.3 0.6 convert_element_type.131
  (3 shorter events, 0.0 us)
Async XLA Ops:
  7.2 20.3 %copy-start = (bf16[1024,128]{1,0:T(8,128)(2,1)S(1)}, bf16[1024,128]{1,0:T(8,128)(2,1)}, u32[]{:S(2)}) copy-start(bf16[1024,128]{1,0:T(8,128)(2,1)} %param.11) | copy-start | bytes 786436
  12.4 15.0 %copy-start.3 = (bf16[1,128,128]{2,1,0:T(8,128)(2,1)S(1)}, bf16[1,128,128]{2,1,0:T(8,128)(2,1)}, u32[]{:S(2)}) copy-start(bf16[1,128,128]{2,1,0:T(8,128)(2,1)} %param.10) | copy-start | bytes 98308
  12.4 29.7 %all-to-all-start = ((bf16[128,2,512]{2,1,0:T(2,128)(2,1)}), bf16[128,2,512]{2,1,0:T(2,128)(2,1)S(1)}, u32[]{:S(2)}, u32[]{:S(2)}) async-start(bf16[128,2,512]{2,1,0:T(2,128)(2,1)} %reshape.118), calls=%async_computation | async-start | bytes 524288 | tf_op jit(solution)/shard_map/all_to_all | solution.py:29
  42.1 20.3 %all-to-all-start.2 = ((bf16[128,2,512]{2,1,0:T(2,128)(2,1)}), bf16[128,2,512]{2,1,0:T(2,128)(2,1)S(1)}, u32[]{:S(2)}, u32[]{:S(2)}) async-start(bf16[128,2,512]{2,1,0:T(2,128)(2,1)} %reshape.120), calls=%async_computation.2 | async-start | bytes 524288 | tf_op jit(solution)/shard_map/all_to_all | solution.py:43
  47.9 0.8 copy-start.2
  48.8 0.8 copy-start.5
  62.4 20.5 %all-to-all-start.1 = ((bf16[128,2,512]{2,1,0:T(2,128)(2,1)}), bf16[128,2,512]{2,1,0:T(2,128)(2,1)S(1)}, u32[]{:S(2)}, u32[]{:S(2)}) async-start(bf16[128,2,512]{2,1,0:T(2,128)(2,1)} %reshape.124), calls=%async_computation.1 | async-start | bytes 524288 | tf_op jit(solution)/shard_map/all_to_all | solution.py:29
  82.9 20.3 %all-to-all-start.3 = ((bf16[128,2,512]{2,1,0:T(2,128)(2,1)}), bf16[128,2,512]{2,1,0:T(2,128)(2,1)S(1)}, u32[]{:S(2)}, u32[]{:S(2)}) async-start(bf16[128,2,512]{2,1,0:T(2,128)(2,1)} %reshape.122), calls=%async_computation.3 | async-start | bytes 524288 | tf_op jit(solution)/shard_map/all_to_all | solution.py:43
  88.4 45.9 %all-reduce.3.cloned.1.call-start = ((), (), s32[]{:S(2)}) async-start(), calls=%async_computation.4 | async-start | bytes 262144 | tf_op jit(solution)/shard_map/psum | solution.py:51
  103.4 1.0 copy-start.1
  105.2 0.8 copy-start.4
  134.3 1.5 %copy-start.8 = (bf16[1,128,128]{2,1,0:T(8,128)(2,1)S(1)}, bf16[1,128,128]{2,1,0:T(8,128)(2,1)}, u32[]{:S(2)}) copy-start(bf16[1,128,128]{2,1,0:T(8,128)(2,1)} %get-tuple-element.25) | copy-start | bytes 98308
  135.8 0.8 copy-start.7
  136.5 0.8 copy-start.6
Sparse Core Ops, SparseCore 0:
  105.4 28.8 all-reduce.2
where the time goes:
time: 146 us; the launch traced here: 145 us
  waiting for transfers between devices  67.8 us (46%)
  starting transfers between devices  31.8 us (22%)
  between operations  14.3 us (10%)
  local copies, waits for them, and re-layouts  12.4 us (8%)
  other arithmetic  10.6 us (7%)
  matrix products  7.82 us (5%)
    psum x1, waiting for transfers between devices, pair_sum(): lax.psum(left_grad.astype(jnp.bfloat16), 'dp').astype(jnp.float32)  27.4 us
    all_to_all x2, waiting for transfers between devices, monarch_forward(): lax.all_to_all(blocks, 'mp', split_axis=2, concat_axis=1, tiled=True)  20.9 us
    all_to_all x2, starting transfers between devices, monarch_forward(): lax.all_to_all(blocks, 'mp', split_axis=2, concat_axis=1, tiled=True)  20.7 us
    all_to_all x2, waiting for transfers between devices, monarch_backward(): lax.all_to_all(back_perm, 'mp', split_axis=1, concat_axis=2, tiled=True)  19.5 us
    all_to_all x2, starting transfers between devices, monarch_backward(): lax.all_to_all(back_perm, 'mp', split_axis=1, concat_axis=2, tiled=True)  11.1 us
    unnamed x28, local copies, waits for them, and re-layouts  8.86 us
    unnamed x4, other arithmetic  8.61 us
  transfers between devices with their start and end apart: 5, of which 5 were waited for; matrix products, arithmetic and copies ran while one was open for 13% of the time, Pallas kernels for 0%

commit v1 on v0

v1 whole, which is shorter than its diff:
```python
import math

import jax
import jax.numpy as jnp
from jax import lax
from jax.experimental import pallas as pl
from jax.experimental.pallas import tpu as pltpu
from jax.sharding import PartitionSpec as P

F32 = jnp.float32
BF16 = jnp.bfloat16
LANES = 128


def gelu_exact(value):
    return 0.5 * value * (1.0 + lax.erf(value / math.sqrt(2.0)))


def gelu_slope(value):
    cumul = 0.5 * (1.0 + lax.erf(value / math.sqrt(2.0)))
    density = jnp.exp(-0.5 * value * value) / math.sqrt(2.0 * math.pi)
    return cumul + value * density


def dot(a, b, ca, cb):
    return lax.dot_general(a, b, (((ca,), (cb,)), ((), ())), preferred_element_type=F32)


def pack(flat):
    return flat.reshape(flat.shape[0], flat.shape[1] // LANES, LANES).astype(BF16)


def unpack(pieces):
    return pieces.astype(F32).reshape(pieces.shape[0], pieces.shape[1] * LANES).astype(BF16)


def send_kernel(x_ref, g_ref, lu_ref, rd_ref, out_ref):
    half = out_ref.shape[1] // 2
    out_ref[:, :half, :] = pack(dot(lu_ref[...], x_ref[...], 0, 1))
    out_ref[:, half:, :] = pack(dot(rd_ref[...], g_ref[...], 1, 1))


def middle_kernel(recv_ref, ru_ref, ld_ref, out_ref, hid_ref, pre_ref):
    half = recv_ref.shape[1] // 2
    ru, ld = ru_ref[...], ld_ref[...]
    pre_act = dot(ru, unpack(recv_ref[:, :half, :]), 0, 0)
    hidden = gelu_exact(pre_act).astype(BF16)
    hid_ref[...] = hidden
    out_ref[:, :half, :] = pack(dot(ld, hidden, 0, 0))
    hidden_back = dot(ld, unpack(recv_ref[:, half:, :]), 1, 0)
    pre_back = (hidden_back * gelu_slope(pre_act)).astype(BF16)
    pre_ref[...] = pre_back
    out_ref[:, half:, :] = pack(dot(ru, pre_back, 1, 0))


def middle_grads_kernel(recv_ref, hid_ref, pre_ref, grads_ref):
    half = recv_ref.shape[1] // 2
    grads_ref[0] = dot(unpack(recv_ref[:, :half, :]), pre_ref[...], 1, 1).astype(BF16)
    grads_ref[1] = dot(hid_ref[...], unpack(recv_ref[:, half:, :]), 1, 1).astype(BF16)


def last_grads_kernel(recv_ref, x_ref, g_ref, grads_ref):
    half = recv_ref.shape[1] // 2
    grads_ref[0] = dot(unpack(recv_ref[:, :half, :]), g_ref[...], 1, 0).astype(BF16)
    grads_ref[1] = dot(unpack(recv_ref[:, half:, :]), x_ref[...], 1, 0).T.astype(BF16)


def last_kernel(recv_ref, lu_ref, rd_ref, out_ref, back_ref):
    half = recv_ref.shape[1] // 2
    out_ref[...] = dot(unpack(recv_ref[:, :half, :]), rd_ref[...], 0, 0).astype(BF16)
    back_ref[...] = dot(unpack(recv_ref[:, half:, :]), lu_ref[...], 0, 1).astype(BF16)


def call(kernel, outs, flops, *args):
    moved = sum(a.size * 2 for a in args) + sum(math.prod(o) * 2 for o in outs)
    single = len(outs) == 1
    shapes = [jax.ShapeDtypeStruct(o, BF16) for o in outs]
    return pl.pallas_call(
        kernel,
        out_shape=shapes[0] if single else shapes,
        compiler_params=pltpu.CompilerParams(vmem_limit_bytes=48 * 1024 * 1024),
        cost_estimate=pl.CostEstimate(flops=flops, bytes_accessed=moved, transcendentals=0),
    )(*args)


def exchange(pieces):
    return lax.all_to_all(pieces, "mp", split_axis=0, concat_axis=0, tiled=True)


def body(activations, left_up, right_up, left_down, right_down, cotangent):
    count, order = activations.shape
    lu, ru, ld, rd = (w.reshape(w.shape[1:]) for w in (left_up, right_up, left_down, right_down))
    message = (order, 2 * count // LANES, LANES)
    unit = 2 * count * order * order
    pair = [(0, 1), (1, 0)]

    sent = call(send_kernel, [message], 2 * unit, activations, cotangent, lu, rd)
    first = exchange(sent)
    sent, hidden, pre_back = call(
        middle_kernel, [message, (order, count), (order, count)], 4 * unit, first, ru, ld
    )
    second = exchange(sent)
    mid = call(middle_grads_kernel, [(2, order, order)], 2 * unit, first, hidden, pre_back)
    mid_other = lax.ppermute(mid, "dp", pair)
    last = call(last_grads_kernel, [(2, order, order)], 2 * unit, second, activations, cotangent)
    last_other = lax.ppermute(last, "dp", pair)
    output, input_grad = call(
        last_kernel, [(count, order), (count, order)], 2 * unit, second, lu, rd
    )
    mid_sum = mid.astype(F32) + mid_other.astype(F32)
    last_sum = last.astype(F32) + last_other.astype(F32)
    return (output, input_grad, last_sum[1:], mid_sum[:1], mid_sum[1:], last_sum[:1])


def solution(mesh):
    tokens, factor = P("dp", "mp"), P("mp", None, None)
    return jax.shard_map(
        body,
        mesh=mesh,
        in_specs=(tokens, factor, factor, factor, factor, tokens),
        out_specs=(tokens, tokens, factor, factor, factor, factor),
        check_vma=False,
    )
```

time: 146 us -> 73.5 us (0.50)
  waiting for transfers between devices: 67.8 us -> 18 us
  blocking collectives: 0 us -> 34.6 us
  starting transfers between devices: 31.8 us -> 10.4 us
  between operations: 14.3 us -> 0.74 us
  other arithmetic: 10.6 us -> 0.03 us
  matrix products: 7.82 us -> 0 us
  local copies, waits for them, and re-layouts: 12.4 us -> 4.76 us
  Pallas kernels: 0 us -> 4.44 us
    all_to_all x0 -> x1, blocking collectives: none -> 34.6 us  [exchange(): return lax.all_to_all(pieces, 'mp', split_axis=0, concat_axis=0, tiled=True)]
    psum x1 -> x0, waiting for transfers between devices: 27.4 us -> none  [pair_sum(): lax.psum(left_grad.astype(jnp.bfloat16), 'dp').astype(jnp.float32)]
    all_to_all x4 -> x1, starting transfers between devices: 31.8 us -> 5.3 us  [exchange(): return lax.all_to_all(pieces, 'mp', split_axis=0, concat_axis=0, tiled=True)]
    all_to_all x4 -> x1, waiting for transfers between devices: 40.4 us -> 14 us  [exchange(): return lax.all_to_all(pieces, 'mp', split_axis=0, concat_axis=0, tiled=True)]
    unnamed x4 -> x0, other arithmetic: 8.61 us -> none
    dot_general x12 -> x0, matrix products: 7.82 us -> none  [the longest x2 1.77 us: monarch_backward(): jnp.einsum('tbj,tjk->jbk', permuted, grad_out, preferred_element_type=jnp...]
    unnamed x28 -> x20, local copies, waits for them, and re-layouts: 8.86 us -> 3.45 us
    ppermute x0 -> x2, starting transfers between devices: none -> 5.09 us  [the longest x1 2.55 us: body(): last_other = lax.ppermute(last, 'dp', pair)]
  transfers between devices with their start and end apart: 5 -> 3, of which waited for: 5 -> 3; matrix products, arithmetic and copies ran while one was open for 13% -> 1% of each run, Pallas kernels for 0% -> 2%
where the time goes in v1:
time: 73.5 us; the launch traced here: 73 us
  blocking collectives  34.6 us (47%)
  waiting for transfers between devices  18 us (24%)
  starting transfers between devices  10.4 us (14%)
  local copies, waits for them, and re-layouts  4.76 us (6%)
  Pallas kernels  4.44 us (6%)
  between operations  0.74 us (1%)
    all_to_all x1, blocking collectives, exchange(): return lax.all_to_all(pieces, 'mp', split_axis=0, concat_axis=0, tiled=True)  34.6 us
    all_to_all x1, waiting for transfers between devices, exchange(): return lax.all_to_all(pieces, 'mp', split_axis=0, concat_axis=0, tiled=True)  14 us
    all_to_all x1, starting transfers between devices, exchange(): return lax.all_to_all(pieces, 'mp', split_axis=0, concat_axis=0, tiled=True)  5.3 us
    pallas_call x5, Pallas kernels, call(): pl.pallas_call(kernel, out_shape=shapes[0] if single else shapes, compile...  4.44 us
    unnamed x20, local copies, waits for them, and re-layouts  3.45 us
    ppermute x1, waiting for transfers between devices, body(): mid_other = lax.ppermute(mid, 'dp', pair)  2.83 us
    ppermute x1, starting transfers between devices, body(): last_other = lax.ppermute(last, 'dp', pair)  2.55 us
    ppermute x1, starting transfers between devices, body(): mid_other = lax.ppermute(mid, 'dp', pair)  2.54 us
  transfers between devices with their start and end apart: 3, of which 3 were waited for; matrix products, arithmetic and copies ran while one was open for 1% of the time, Pallas kernels for 2%

profile of v1, /device:TPU:1, one launch (start us, length us, event | category | flops | bytes accessed | tf_op | source)
XLA Modules:
  0.0 73.0 jit_solution(7936589766018835147)
XLA Ops:
  0.6 0.0 copy-start
  0.6 0.9 %copy-done = bf16[1024,128]{1,0:T(8,128)(2,1)S(1)} copy-done((bf16[1024,128]{1,0:T(8,128)(2,1)S(1)}, bf16[1024,128]{1,0:T(8,128)(2,1)}, u32[]{:S(2)}) %copy-start) | copy-done | bytes 262168
  1.6 0.0 copy-start.2
  1.6 0.9 %copy-done.2 = bf16[1024,128]{1,0:T(8,128)(2,1)S(1)} copy-done((bf16[1024,128]{1,0:T(8,128)(2,1)S(1)}, bf16[1024,128]{1,0:T(8,128)(2,1)}, u32[]{:S(2)}) %copy-start.2) | copy-done | bytes 262168
  2.5 0.0 copy-start.4
  2.5 0.8 %copy-done.4 = bf16[1,128,128]{2,1,0:T(8,128)(2,1)S(1)} copy-done((bf16[1,128,128]{2,1,0:T(8,128)(2,1)S(1)}, bf16[1,128,128]{2,1,0:T(8,128)(2,1)}, u32[]{:S(2)}) %copy-start.4) | copy-done | bytes 32792
  3.3 0.0 copy-start.6
  3.3 0.8 %copy-done.6 = bf16[1,128,128]{2,1,0:T(8,128)(2,1)S(1)} copy-done((bf16[1,128,128]{2,1,0:T(8,128)(2,1)S(1)}, bf16[1,128,128]{2,1,0:T(8,128)(2,1)}, u32[]{:S(2)}) %copy-start.6) | copy-done | bytes 32792
  4.1 0.4 shard_map.109
  4.5 0.0 copy-start.8
  4.5 0.0 copy-start.9
  4.5 34.6 %all_to_all.10.recv_ref = bf16[128,16,128]{2,1,0:T(8,128)(2,1)S(1)} all-to-all(bf16[128,16,128]{2,1,0:T(8,128)(2,1)S(1)} %shard_map.109), channel_id=1, replica_groups=mesh['dp'=2,'mp'=128] {'mp'}, dimensions={0} | all-to-all | bytes 1048576 | tf_op jit(solution)/shard_map/all_to_all | solution.py:87
  39.1 0.0 copy-done.8
  39.1 0.0 copy-done.9
  39.1 1.9 %shard_map.110 = (bf16[128,16,128]{2,1,0:T(8,128)(2,1)}, bf16[128,1024]{1,0:T(8,128)(2,1)S(1)}, bf16[128,1024]{1,0:T(8,128)(2,1)S(1)}) custom-call(bf16[128,16,128]{2,1,0:T(8,128)(2,1)S(1)} %all_to_all.10.recv_ref, bf16[128,128]{1,0:T(8,128)(2,1)S(1)} %bitcast.8, bf16[128,128]{1,0:T(8,128)(2,1)S(1)} %bitcast.9), custom_call_target="tpu_custom_call" | custom-call | flops 134217728 | bytes 1638400 | tf_op jit(solution)/shard_map/pallas_call | solution.py:78
  41.0 5.3 %all-to-all-start.1 = ((bf16[128,16,128]{2,1,0:T(8,128)(2,1)}), bf16[128,16,128]{2,1,0:T(8,128)(2,1)S(1)}, u32[]{:S(2)}, u32[]{:S(2)}) async-start(bf16[128,16,128]{2,1,0:T(8,128)(2,1)} %get-tuple-element.11), calls=%async_computation.1 | async-start | bytes 1048576 | tf_op jit(solution)/shard_map/all_to_all | solution.py:87
  46.3 0.0 copy-start.3
  46.4 0.4 shard_map.113
  46.8 0.0 copy-start.1
  46.8 2.5 %collective-permute-start.1 = (bf16[2,128,128]{2,1,0:T(8,128)(2,1)S(1)}, bf16[2,128,128]{2,1,0:T(8,128)(2,1)S(1)}, u32[]{:S(2)}, u32[]{:S(2)}) collective-permute-start(bf16[2,128,128]{2,1,0:T(8,128)(2,1)S(1)} %shard_map.113), channel_id=1, source_target_pairs={{0,128},{128,0},{1,129},{129,1},{2,130},{130,2},{3,131},{131,3},{4... | collective-permute-start | bytes 196616 | tf_op jit(solution)/shard_map/ppermute | solution.py:104
  49.3 2.8 %collective-permute-done.1 = bf16[2,128,128]{2,1,0:T(8,128)(2,1)S(1)} collective-permute-done((bf16[2,128,128]{2,1,0:T(8,128)(2,1)S(1)}, bf16[2,128,128]{2,1,0:T(8,128)(2,1)S(1)}, u32[]{:S(2)}, u32[]{:S(2)}) %collective-permute-start.1) | collective-permute-done | bytes 65568 | tf_op jit(solution)/shard_map/ppermute | solution.py:104
  52.2 14.0 %all-to-all-done.1.recv_ref = bf16[128,16,128]{2,1,0:T(8,128)(2,1)S(1)} async-done(((bf16[128,16,128]{2,1,0:T(8,128)(2,1)}), bf16[128,16,128]{2,1,0:T(8,128)(2,1)S(1)}, u32[]{:S(2)}, u32[]{:S(2)}) %all-to-all-start.1) | async-done | bytes 524320 | tf_op jit(solution)/shard_map/all_to_all | solution.py:87
  66.2 0.0 copy-done.3
  66.2 0.0 copy-done.1
  66.2 0.5 shard_map.112
  66.7 0.0 copy-start.5
  66.7 0.0 copy-start.7
  66.7 2.5 %collective-permute-start = (bf16[2,128,128]{2,1,0:T(8,128)(2,1)S(1)}, bf16[2,128,128]{2,1,0:T(8,128)(2,1)S(1)}, u32[]{:S(2)}, u32[]{:S(2)}) collective-permute-start(bf16[2,128,128]{2,1,0:T(8,128)(2,1)S(1)} %shard_map.112), channel_id=1, source_target_pairs={{0,128},{128,0},{1,129},{129,1},{2,130},{130,2},{3,131},{131,3},{4... | collective-permute-start | bytes 196616 | tf_op jit(solution)/shard_map/ppermute | solution.py:106
  69.3 0.7 fusion.1
  69.9 0.0 copy-done.5
  69.9 0.0 copy-done.7
  69.9 1.3 %shard_map.111 = (bf16[1024,128]{1,0:T(8,128)(2,1)}, bf16[1024,128]{1,0:T(8,128)(2,1)}) custom-call(bf16[128,16,128]{2,1,0:T(8,128)(2,1)S(1)} %all-to-all-done.1.recv_ref, bf16[128,128]{1,0:T(8,128)(2,1)S(1)} %bitcast.5, bf16[128,128]{1,0:T(8,128)(2,1)S(1)} %bitcast.7), custom_call_target="tpu_custom_call" | custom-call | flops 67108864 | bytes 1114112 | tf_op jit(solution)/shard_map/pallas_call | solution.py:78
  71.2 1.2 %collective-permute-done = bf16[2,128,128]{2,1,0:T(8,128)(2,1)S(1)} collective-permute-done((bf16[2,128,128]{2,1,0:T(8,128)(2,1)S(1)}, bf16[2,128,128]{2,1,0:T(8,128)(2,1)S(1)}, u32[]{:S(2)}, u32[]{:S(2)}) %collective-permute-start) | collective-permute-done | bytes 65568 | tf_op jit(solution)/shard_map/ppermute | solution.py:106
  72.4 0.7 fusion
  (2 shorter events, 0.0 us)
Async XLA Ops:
  0.6 1.0 %copy-start = (bf16[1024,128]{1,0:T(8,128)(2,1)S(1)}, bf16[1024,128]{1,0:T(8,128)(2,1)}, u32[]{:S(2)}) copy-start(bf16[1024,128]{1,0:T(8,128)(2,1)} %x_ref.3) | copy-start | bytes 786436
  1.6 0.9 %copy-start.2 = (bf16[1024,128]{1,0:T(8,128)(2,1)S(1)}, bf16[1024,128]{1,0:T(8,128)(2,1)}, u32[]{:S(2)}) copy-start(bf16[1024,128]{1,0:T(8,128)(2,1)} %g_ref.3) | copy-start | bytes 786436
  2.5 0.8 %copy-start.4 = (bf16[1,128,128]{2,1,0:T(8,128)(2,1)S(1)}, bf16[1,128,128]{2,1,0:T(8,128)(2,1)}, u32[]{:S(2)}) copy-start(bf16[1,128,128]{2,1,0:T(8,128)(2,1)} %param.7) | copy-start | bytes 98308
  3.3 0.8 %copy-start.6 = (bf16[1,128,128]{2,1,0:T(8,128)(2,1)S(1)}, bf16[1,128,128]{2,1,0:T(8,128)(2,1)}, u32[]{:S(2)}) copy-start(bf16[1,128,128]{2,1,0:T(8,128)(2,1)} %param.10) | copy-start | bytes 98308
  4.5 34.7 %copy-start.8 = (bf16[1,128,128]{2,1,0:T(8,128)(2,1)S(1)}, bf16[1,128,128]{2,1,0:T(8,128)(2,1)}, u32[]{:S(2)}) copy-start(bf16[1,128,128]{2,1,0:T(8,128)(2,1)} %param.8) | copy-start | bytes 98308
  4.5 34.7 %copy-start.9 = (bf16[1,128,128]{2,1,0:T(8,128)(2,1)S(1)}, bf16[1,128,128]{2,1,0:T(8,128)(2,1)}, u32[]{:S(2)}) copy-start(bf16[1,128,128]{2,1,0:T(8,128)(2,1)} %param.9) | copy-start | bytes 98308
  41.0 25.2 %all-to-all-start.1 = ((bf16[128,16,128]{2,1,0:T(8,128)(2,1)}), bf16[128,16,128]{2,1,0:T(8,128)(2,1)S(1)}, u32[]{:S(2)}, u32[]{:S(2)}) async-start(bf16[128,16,128]{2,1,0:T(8,128)(2,1)} %get-tuple-element.11), calls=%async_computation.1 | async-start | bytes 1048576 | tf_op jit(solution)/shard_map/all_to_all | solution.py:87
  46.3 19.9 %copy-start.3 = (bf16[1024,128]{1,0:T(8,128)(2,1)S(1)}, bf16[1024,128]{1,0:T(8,128)(2,1)}, u32[]{:S(2)}) copy-start(bf16[1024,128]{1,0:T(8,128)(2,1)} %g_ref.3) | copy-start | bytes 786436
  46.8 19.4 %copy-start.1 = (bf16[1024,128]{1,0:T(8,128)(2,1)S(1)}, bf16[1024,128]{1,0:T(8,128)(2,1)}, u32[]{:S(2)}) copy-start(bf16[1024,128]{1,0:T(8,128)(2,1)} %x_ref.3) | copy-start | bytes 786436
  46.8 5.4 %collective-permute-start.1 = (bf16[2,128,128]{2,1,0:T(8,128)(2,1)S(1)}, bf16[2,128,128]{2,1,0:T(8,128)(2,1)S(1)}, u32[]{:S(2)}, u32[]{:S(2)}) collective-permute-start(bf16[2,128,128]{2,1,0:T(8,128)(2,1)S(1)} %shard_map.113), channel_id=1, source_target_pairs={{0,128},{128,0},{1,129},{129,1},{2,130},{130,2},{3,131},{131,3},{4... | collective-permute-start | bytes 196616 | tf_op jit(solution)/shard_map/ppermute | solution.py:104
  66.7 3.2 %copy-start.5 = (bf16[1,128,128]{2,1,0:T(8,128)(2,1)S(1)}, bf16[1,128,128]{2,1,0:T(8,128)(2,1)}, u32[]{:S(2)}) copy-start(bf16[1,128,128]{2,1,0:T(8,128)(2,1)} %param.7) | copy-start | bytes 98308
  66.7 3.2 %copy-start.7 = (bf16[1,128,128]{2,1,0:T(8,128)(2,1)S(1)}, bf16[1,128,128]{2,1,0:T(8,128)(2,1)}, u32[]{:S(2)}) copy-start(bf16[1,128,128]{2,1,0:T(8,128)(2,1)} %param.10) | copy-start | bytes 98308
  66.7 5.6 %collective-permute-start = (bf16[2,128,128]{2,1,0:T(8,128)(2,1)S(1)}, bf16[2,128,128]{2,1,0:T(8,128)(2,1)S(1)}, u32[]{:S(2)}, u32[]{:S(2)}) collective-permute-start(bf16[2,128,128]{2,1,0:T(8,128)(2,1)S(1)} %shard_map.112), channel_id=1, source_target_pairs={{0,128},{128,0},{1,129},{129,1},{2,130},{130,2},{3,131},{131,3},{4... | collective-permute-start | bytes 196616 | tf_op jit(solution)/shard_map/ppermute | solution.py:106

commit v2 on v1

v2 whole, which is shorter than its diff:
```python
import functools
import math

import jax
import jax.numpy as jnp
import numpy as np
from jax import lax
from jax.experimental import pallas as pl
from jax.experimental.pallas import tpu as pltpu
from jax.sharding import PartitionSpec as P

F32 = jnp.float32
BF16 = jnp.bfloat16
LANES = 128
MP_AXES = (4, 2, 8, 2)
PART_VMEM, WHOLE_VMEM = 48 * 1024 * 1024, 60 * 1024 * 1024
IN_HBM = pl.BlockSpec(memory_space=pltpu.HBM)
IN_VMEM = pl.BlockSpec(memory_space=pltpu.VMEM)


def gelu_exact(value):
    return 0.5 * value * (1.0 + lax.erf(value / math.sqrt(2.0)))


def gelu_slope(value):
    cumul = 0.5 * (1.0 + lax.erf(value / math.sqrt(2.0)))
    density = jnp.exp(-0.5 * value * value) / math.sqrt(2.0 * math.pi)
    return cumul + value * density


def dot(a, b, ca, cb):
    return lax.dot_general(a, b, (((ca,), (cb,)), ((), ())), preferred_element_type=F32)


def runs_of(order):
    runs = []
    for position, member in enumerate(order):
        if runs and member == runs[-1][1] + runs[-1][2]:
            runs[-1][2] += 1
        else:
            runs.append([position, member, 1])
    return sorted((tuple(run) for run in runs), key=lambda run: run[1])


def put(ref, half, runs, flat):
    rows = ref.shape[1] // 2
    pieces = flat.astype(BF16).reshape(flat.shape[0], rows, LANES)
    for position, member, length in runs:
        ref[pl.ds(position, length), pl.ds(half * rows, rows), :] = pieces[member : member + length]


def take(ref, half, runs):
    rows = ref.shape[1] // 2
    pieces = [ref[pl.ds(p, length), pl.ds(half * rows, rows), :] for p, _, length in runs]
    pieces = pieces[0] if len(pieces) == 1 else jnp.concatenate(pieces, axis=0)
    return pieces.reshape(pieces.shape[0], rows * LANES)


def ship(half, out_ref, out_hbm, sems):
    rows = out_ref.shape[1] // 2
    part = pl.ds(half * rows, rows)
    return pltpu.make_async_copy(out_ref.at[:, part, :], out_hbm.at[:, part, :], sems.at[half])


def send_kernel(
    runs, x_hbm, g_hbm, lu_hbm, rd_hbm, out_hbm, x_ref, g_ref, lu_ref, rd_ref, out_ref, in_sems, sems
):
    pairs = ((lu_hbm, lu_ref), (x_hbm, x_ref), (rd_hbm, rd_ref), (g_hbm, g_ref))
    copies = [pltpu.make_async_copy(a, b, in_sems.at[i]) for i, (a, b) in enumerate(pairs)]
    for copy in copies:
        copy.start()
    copies[0].wait()
    copies[1].wait()
    put(out_ref, 0, runs, dot(lu_ref[...], x_ref[...], 0, 1))
    first = ship(0, out_ref, out_hbm, sems)
    first.start()
    copies[2].wait()
    copies[3].wait()
    put(out_ref, 1, runs, dot(rd_ref[...], g_ref[...], 1, 1))
    second = ship(1, out_ref, out_hbm, sems)
    second.start()
    first.wait()
    second.wait()


def middle_kernel(came, runs, recv_ref, ru_ref, ld_ref, out_hbm, hid_ref, pre_ref, out_ref, sems):
    ru, ld = ru_ref[...], ld_ref[...]
    pre_act = dot(ru, take(recv_ref, 0, came), 0, 0)
    hidden = gelu_exact(pre_act).astype(BF16)
    put(out_ref, 0, runs, dot(ld, hidden, 0, 0))
    first = ship(0, out_ref, out_hbm, sems)
    first.start()
    hid_ref[...] = hidden
    hidden_back = dot(ld, take(recv_ref, 1, came), 1, 0)
    pre_back = (hidden_back * gelu_slope(pre_act)).astype(BF16)
    put(out_ref, 1, runs, dot(ru, pre_back, 1, 0))
    second = ship(1, out_ref, out_hbm, sems)
    second.start()
    pre_ref[...] = pre_back
    first.wait()
    second.wait()


def middle_grads_kernel(came, recv_ref, hid_ref, pre_ref, grads_ref):
    grads_ref[0] = dot(take(recv_ref, 0, came), pre_ref[...], 1, 1).astype(BF16)
    grads_ref[1] = dot(hid_ref[...], take(recv_ref, 1, came), 1, 1).astype(BF16)


def last_grads_kernel(came, recv_ref, x_ref, g_ref, grads_ref):
    grads_ref[0] = dot(take(recv_ref, 0, came), g_ref[...], 1, 0).astype(BF16)
    grads_ref[1] = dot(take(recv_ref, 1, came), x_ref[...], 1, 0).T.astype(BF16)


def last_kernel(came, recv_ref, lu_ref, rd_ref, out_ref, back_ref):
    out_ref[...] = dot(take(recv_ref, 0, came), rd_ref[...], 0, 0).astype(BF16)
    back_ref[...] = dot(take(recv_ref, 1, came), lu_ref[...], 0, 1).astype(BF16)


def call(kernel, outs, flops, *args, scratch=(), vmem=PART_VMEM, **specs):
    moved = sum(a.size * 2 for a in args) + sum(math.prod(o) * 2 for o in outs)
    single = len(outs) == 1
    shapes = [jax.ShapeDtypeStruct(o, BF16) for o in outs]
    return pl.pallas_call(
        kernel,
        out_shape=shapes[0] if single else shapes,
        scratch_shapes=list(scratch),
        compiler_params=pltpu.CompilerParams(vmem_limit_bytes=vmem),
        cost_estimate=pl.CostEstimate(flops=flops, bytes_accessed=moved, transcendentals=0),
        **specs,
    )(*args)


def exchange(pieces, order):
    return lax.all_to_all(
        pieces, "mp", split_axis=0, concat_axis=0, tiled=True, axis_index_groups=[list(order)]
    )


def body(order, activations, left_up, right_up, left_down, right_down, cotangent):
    count, size = activations.shape
    lu, ru, ld, rd = (w.reshape(w.shape[1:]) for w in (left_up, right_up, left_down, right_down))
    message = (size, 2 * count // LANES, LANES)
    square, wide, tall = (size, size), (size, count), (count, size)
    unit = 2 * count * size * size
    pair = [(0, 1), (1, 0)]
    runs = runs_of(order)
    dma = pltpu.SemaphoreType.DMA

    sent = call(
        functools.partial(send_kernel, runs),
        [message],
        2 * unit,
        activations,
        cotangent,
        lu,
        rd,
        vmem=WHOLE_VMEM,
        scratch=[pltpu.VMEM(s, BF16) for s in (tall, tall, square, square, message)]
        + [dma((4,)), dma((2,))],
        in_specs=[IN_HBM] * 4,
        out_specs=IN_HBM,
    )
    first = exchange(sent, order)
    sent, hidden, pre_back = call(
        functools.partial(middle_kernel, runs, runs),
        [message, wide, wide],
        4 * unit,
        first,
        ru,
        ld,
        scratch=[pltpu.VMEM(message, BF16), dma((2,))],
        out_specs=[IN_HBM, IN_VMEM, IN_VMEM],
    )
    second = exchange(sent, order)
    mid = call(
        functools.partial(middle_grads_kernel, runs),
        [(2, *square)],
        2 * unit,
        first,
        hidden,
        pre_back,
    )
    mid_other = lax.ppermute(mid, "dp", pair)
    last = call(
        functools.partial(last_grads_kernel, runs),
        [(2, *square)],
        2 * unit,
        second,
        activations,
        cotangent,
    )
    last_other = lax.ppermute(last, "dp", pair)
    output, input_grad = call(
        functools.partial(last_kernel, runs), [tall, tall], 2 * unit, second, lu, rd
    )
    mid_sum = mid.astype(F32) + mid_other.astype(F32)
    last_sum = last.astype(F32) + last_other.astype(F32)
    return (output, input_grad, last_sum[1:], mid_sum[:1], mid_sum[1:], last_sum[:1])


def group_order():
    members = np.arange(math.prod(MP_AXES)).reshape(MP_AXES)
    far = [extent // 2 for extent in MP_AXES[:3]]
    return tuple(int(m) for m in np.roll(members, [-f for f in far], (0, 1, 2)).reshape(-1))


def solution(mesh):
    tokens, factor = P("dp", "mp"), P("mp", None, None)
    order = group_order()
    return jax.shard_map(
        functools.partial(body, order),
        mesh=mesh,
        in_specs=(tokens, factor, factor, factor, factor, tokens),
        out_specs=(tokens, tokens, factor, factor, factor, factor),
        check_vma=False,
    )
```

time: 73.5 us -> 65.4 us (0.89)
  waiting for transfers between devices: 18 us -> 8.96 us
  starting transfers between devices: 10.4 us -> 18.5 us
  blocking collectives: 34.6 us -> 29.5 us
  local copies, waits for them, and re-layouts: 4.76 us -> 1.35 us
  Pallas kernels: 4.44 us -> 5.88 us
    all_to_all x1, waiting for transfers between devices: 14 us -> 5.1 us  [exchange(): lax.all_to_all(pieces, 'mp', split_axis=0, concat_axis=0, tiled=True, axi...]
    all_to_all x1, starting transfers between devices: 5.3 us -> 13.4 us  [exchange(): lax.all_to_all(pieces, 'mp', split_axis=0, concat_axis=0, tiled=True, axi...]
    all_to_all x1, blocking collectives: 34.6 us -> 29.5 us  [exchange(): lax.all_to_all(pieces, 'mp', split_axis=0, concat_axis=0, tiled=True, axi...]
    unnamed x20 -> x12, local copies, waits for them, and re-layouts: 3.45 us -> 0.04 us
    pallas_call x5, Pallas kernels: 4.44 us -> 5.88 us  [call(): pl.pallas_call(kernel, out_shape=shapes[0] if single else shapes, scratch...]
    ppermute x1, waiting for transfers between devices: 1.18 us -> 0.31 us  [body(): last_other = lax.ppermute(last, 'dp', pair)]
where the time goes in v2:
time: 65.4 us; the launch traced here: 64.9 us
  blocking collectives  29.5 us (45%)
  starting transfers between devices  18.5 us (28%)
  waiting for transfers between devices  8.96 us (14%)
  Pallas kernels  5.88 us (9%)
  local copies, waits for them, and re-layouts  1.35 us (2%)
  between operations  0.73 us (1%)
    all_to_all x1, blocking collectives, exchange(): lax.all_to_all(pieces, 'mp', split_axis=0, concat_axis=0, tiled=True, axi...  29.5 us
    all_to_all x1, starting transfers between devices, exchange(): lax.all_to_all(pieces, 'mp', split_axis=0, concat_axis=0, tiled=True, axi...  13.4 us
    pallas_call x5, Pallas kernels, call(): pl.pallas_call(kernel, out_shape=shapes[0] if single else shapes, scratch...  5.88 us
    all_to_all x1, waiting for transfers between devices, exchange(): lax.all_to_all(pieces, 'mp', split_axis=0, concat_axis=0, tiled=True, axi...  5.1 us
    ppermute x1, waiting for transfers between devices, body(): mid_other = lax.ppermute(mid, 'dp', pair)  3.55 us
    ppermute x1, starting transfers between devices, body(): mid_other = lax.ppermute(mid, 'dp', pair)  2.57 us
    ppermute x1, starting transfers between devices, body(): last_other = lax.ppermute(last, 'dp', pair)  2.57 us
  transfers between devices with their start and end apart: 3, of which 3 were waited for; matrix products, arithmetic and copies ran while one was open for 1% of the time, Pallas kernels for 2%

profile of v2, /device:TPU:1, one launch (start us, length us, event | category | flops | bytes accessed | tf_op | source)
XLA Modules:
  0.0 64.9 jit_solution(40342484277643596)
XLA Ops:
  0.6 2.3 %shard_map.109 = bf16[128,16,128]{2,1,0:T(8,128)(2,1)} custom-call(bf16[1024,128]{1,0:T(8,128)(2,1)} %x_ref.1, bf16[1024,128]{1,0:T(8,128)(2,1)} %g_ref.1, bf16[128,128]{1,0:T(8,128)(2,1)} %bitcast.4, bf16[128,128]{1,0:T(8,128)(2,1)} %bitcast.6), custom_call_target="tpu_custom_call" | custom-call | flops 67108864 | bytes 1114112 | tf_op jit(solution)/shard_map/pallas_call | solution.py:123
  2.9 0.0 copy-start.4
  2.9 0.0 copy-start.5
  3.0 29.5 %all_to_all.10.recv_ref = bf16[128,16,128]{2,1,0:T(8,128)(2,1)S(1)} all-to-all(bf16[128,16,128]{2,1,0:T(8,128)(2,1)} %shard_map.109), channel_id=1, replica_groups={{88,89,90,91,92,93,94,95,80,81,82,83,84,85,86,87,72,73,74,75,76,77,78,7..., dimensions={0} | all-to-all | bytes 1048576 | tf_op jit(solution)/shard_map/all_to_all | solution.py:134
  32.4 0.0 copy-done.4
  32.4 0.0 copy-done.5
  32.5 1.7 %shard_map.110 = (bf16[128,16,128]{2,1,0:T(8,128)(2,1)}, bf16[128,1024]{1,0:T(8,128)(2,1)S(1)}, bf16[128,1024]{1,0:T(8,128)(2,1)S(1)}) custom-call(bf16[128,16,128]{2,1,0:T(8,128)(2,1)S(1)} %all_to_all.10.recv_ref, bf16[128,128]{1,0:T(8,128)(2,1)S(1)} %bitcast.8, bf16[128,128]{1,0:T(8,128)(2,1)S(1)} %bitcast.9), custom_call_target="tpu_custom_call" | custom-call | flops 134217728 | bytes 1638400 | tf_op jit(solution)/shard_map/pallas_call | solution.py:123
  34.1 13.4 %all-to-all-start.1 = ((bf16[128,16,128]{2,1,0:T(8,128)(2,1)}), bf16[128,16,128]{2,1,0:T(8,128)(2,1)S(1)}, u32[]{:S(2)}, u32[]{:S(2)}) async-start(bf16[128,16,128]{2,1,0:T(8,128)(2,1)} %get-tuple-element.11), calls=%async_computation.1 | async-start | bytes 1048576 | tf_op jit(solution)/shard_map/all_to_all | solution.py:134
  47.5 0.0 copy-start.1
  47.5 0.3 shard_map.113
  47.9 0.0 copy-start
  47.9 2.6 %collective-permute-start.1 = (bf16[2,128,128]{2,1,0:T(8,128)(2,1)S(1)}, bf16[2,128,128]{2,1,0:T(8,128)(2,1)S(1)}, u32[]{:S(2)}, u32[]{:S(2)}) collective-permute-start(bf16[2,128,128]{2,1,0:T(8,128)(2,1)S(1)} %shard_map.113), channel_id=1, source_target_pairs={{0,128},{128,0},{1,129},{129,1},{2,130},{130,2},{3,131},{131,3},{4... | collective-permute-start | bytes 196616 | tf_op jit(solution)/shard_map/ppermute | solution.py:183
  50.4 3.6 %collective-permute-done.1 = bf16[2,128,128]{2,1,0:T(8,128)(2,1)S(1)} collective-permute-done((bf16[2,128,128]{2,1,0:T(8,128)(2,1)S(1)}, bf16[2,128,128]{2,1,0:T(8,128)(2,1)S(1)}, u32[]{:S(2)}, u32[]{:S(2)}) %collective-permute-start.1) | collective-permute-done | bytes 65568 | tf_op jit(solution)/shard_map/ppermute | solution.py:183
  54.0 5.1 %all-to-all-done.1.recv_ref = bf16[128,16,128]{2,1,0:T(8,128)(2,1)S(1)} async-done(((bf16[128,16,128]{2,1,0:T(8,128)(2,1)}), bf16[128,16,128]{2,1,0:T(8,128)(2,1)S(1)}, u32[]{:S(2)}, u32[]{:S(2)}) %all-to-all-start.1) | async-done | bytes 524320 | tf_op jit(solution)/shard_map/all_to_all | solution.py:134
  59.1 0.0 copy-done.1
  59.1 0.0 copy-done
  59.1 0.4 shard_map.112
  59.5 0.0 copy-start.2
  59.5 0.0 copy-start.3
  59.5 2.6 %collective-permute-start = (bf16[2,128,128]{2,1,0:T(8,128)(2,1)S(1)}, bf16[2,128,128]{2,1,0:T(8,128)(2,1)S(1)}, u32[]{:S(2)}, u32[]{:S(2)}) collective-permute-start(bf16[2,128,128]{2,1,0:T(8,128)(2,1)S(1)} %shard_map.112), channel_id=1, source_target_pairs={{0,128},{128,0},{1,129},{129,1},{2,130},{130,2},{3,131},{131,3},{4... | collective-permute-start | bytes 196616 | tf_op jit(solution)/shard_map/ppermute | solution.py:192
  62.1 0.7 %fusion.1 = (f32[1,128,128]{2,1,0:T(8,128)}, f32[1,128,128]{2,1,0:T(8,128)}) fusion(f32[2,128,128]{2,1,0:T(8,128)S(1)} %convert_add_fusion), kind=kLoop, calls=%fused_computation.3 | loop fusion | bytes 262144 | tf_op jit(solution)/shard_map/slice | solution.py:198
  62.8 0.0 copy-done.2
  62.8 0.0 copy-done.3
  62.8 1.2 %shard_map.111 = (bf16[1024,128]{1,0:T(8,128)(2,1)}, bf16[1024,128]{1,0:T(8,128)(2,1)}) custom-call(bf16[128,16,128]{2,1,0:T(8,128)(2,1)S(1)} %all-to-all-done.1.recv_ref, bf16[128,128]{1,0:T(8,128)(2,1)S(1)} %bitcast.5, bf16[128,128]{1,0:T(8,128)(2,1)S(1)} %bitcast.7), custom_call_target="tpu_custom_call" | custom-call | flops 67108864 | bytes 1114112 | tf_op jit(solution)/shard_map/pallas_call | solution.py:123
  63.9 0.3 collective-permute-done
  64.3 0.7 %fusion = (f32[1,128,128]{2,1,0:T(8,128)}, f32[1,128,128]{2,1,0:T(8,128)}) fusion(f32[2,128,128]{2,1,0:T(8,128)S(1)} %convert_add_fusion.1), kind=kLoop, calls=%fused_computation.2 | loop fusion | bytes 262144 | tf_op jit(solution)/shard_map/slice | solution.py:198
  (2 shorter events, 0.0 us)
Async XLA Ops:
  2.9 29.5 %copy-start.4 = (bf16[1,128,128]{2,1,0:T(8,128)(2,1)S(1)}, bf16[1,128,128]{2,1,0:T(8,128)(2,1)}, u32[]{:S(2)}) copy-start(bf16[1,128,128]{2,1,0:T(8,128)(2,1)} %param.8) | copy-start | bytes 98308
  2.9 29.5 %copy-start.5 = (bf16[1,128,128]{2,1,0:T(8,128)(2,1)S(1)}, bf16[1,128,128]{2,1,0:T(8,128)(2,1)}, u32[]{:S(2)}) copy-start(bf16[1,128,128]{2,1,0:T(8,128)(2,1)} %param.9) | copy-start | bytes 98308
  34.1 25.0 %all-to-all-start.1 = ((bf16[128,16,128]{2,1,0:T(8,128)(2,1)}), bf16[128,16,128]{2,1,0:T(8,128)(2,1)S(1)}, u32[]{:S(2)}, u32[]{:S(2)}) async-start(bf16[128,16,128]{2,1,0:T(8,128)(2,1)} %get-tuple-element.11), calls=%async_computation.1 | async-start | bytes 1048576 | tf_op jit(solution)/shard_map/all_to_all | solution.py:134
  47.5 11.6 %copy-start.1 = (bf16[1024,128]{1,0:T(8,128)(2,1)S(1)}, bf16[1024,128]{1,0:T(8,128)(2,1)}, u32[]{:S(2)}) copy-start(bf16[1024,128]{1,0:T(8,128)(2,1)} %g_ref.1) | copy-start | bytes 786436
  47.9 11.3 %copy-start = (bf16[1024,128]{1,0:T(8,128)(2,1)S(1)}, bf16[1024,128]{1,0:T(8,128)(2,1)}, u32[]{:S(2)}) copy-start(bf16[1024,128]{1,0:T(8,128)(2,1)} %x_ref.1) | copy-start | bytes 786436
  47.9 6.1 %collective-permute-start.1 = (bf16[2,128,128]{2,1,0:T(8,128)(2,1)S(1)}, bf16[2,128,128]{2,1,0:T(8,128)(2,1)S(1)}, u32[]{:S(2)}, u32[]{:S(2)}) collective-permute-start(bf16[2,128,128]{2,1,0:T(8,128)(2,1)S(1)} %shard_map.113), channel_id=1, source_target_pairs={{0,128},{128,0},{1,129},{129,1},{2,130},{130,2},{3,131},{131,3},{4... | collective-permute-start | bytes 196616 | tf_op jit(solution)/shard_map/ppermute | solution.py:183
  59.5 3.2 %copy-start.2 = (bf16[1,128,128]{2,1,0:T(8,128)(2,1)S(1)}, bf16[1,128,128]{2,1,0:T(8,128)(2,1)}, u32[]{:S(2)}) copy-start(bf16[1,128,128]{2,1,0:T(8,128)(2,1)} %param.7) | copy-start | bytes 98308
  59.5 3.2 %copy-start.3 = (bf16[1,128,128]{2,1,0:T(8,128)(2,1)S(1)}, bf16[1,128,128]{2,1,0:T(8,128)(2,1)}, u32[]{:S(2)}) copy-start(bf16[1,128,128]{2,1,0:T(8,128)(2,1)} %param.10) | copy-start | bytes 98308
  59.5 4.7 %collective-permute-start = (bf16[2,128,128]{2,1,0:T(8,128)(2,1)S(1)}, bf16[2,128,128]{2,1,0:T(8,128)(2,1)S(1)}, u32[]{:S(2)}, u32[]{:S(2)}) collective-permute-start(bf16[2,128,128]{2,1,0:T(8,128)(2,1)S(1)} %shard_map.112), channel_id=1, source_target_pairs={{0,128},{128,0},{1,129},{129,1},{2,130},{130,2},{3,131},{131,3},{4... | collective-permute-start | bytes 196616 | tf_op jit(solution)/shard_map/ppermute | solution.py:192

commit v3 on v2

--- a/solution.py
+++ b/solution.py
@@ -13,7 +13,6 @@
 BF16 = jnp.bfloat16
 LANES = 128
 MP_AXES = (4, 2, 8, 2)
-PART_VMEM, WHOLE_VMEM = 48 * 1024 * 1024, 60 * 1024 * 1024
 IN_HBM = pl.BlockSpec(memory_space=pltpu.HBM)
 IN_VMEM = pl.BlockSpec(memory_space=pltpu.VMEM)
 
@@ -62,25 +61,17 @@
     return pltpu.make_async_copy(out_ref.at[:, part, :], out_hbm.at[:, part, :], sems.at[half])
 
 
-def send_kernel(
-    runs, x_hbm, g_hbm, lu_hbm, rd_hbm, out_hbm, x_ref, g_ref, lu_ref, rd_ref, out_ref, in_sems, sems
-):
+def send_kernel(runs, x_hbm, g_hbm, lu_hbm, rd_hbm, out_ref, x_ref, g_ref, lu_ref, rd_ref, sems):
     pairs = ((lu_hbm, lu_ref), (x_hbm, x_ref), (rd_hbm, rd_ref), (g_hbm, g_ref))
-    copies = [pltpu.make_async_copy(a, b, in_sems.at[i]) for i, (a, b) in enumerate(pairs)]
+    copies = [pltpu.make_async_copy(a, b, sems.at[i]) for i, (a, b) in enumerate(pairs)]
     for copy in copies:
         copy.start()
     copies[0].wait()
     copies[1].wait()
     put(out_ref, 0, runs, dot(lu_ref[...], x_ref[...], 0, 1))
-    first = ship(0, out_ref, out_hbm, sems)
-    first.start()
     copies[2].wait()
     copies[3].wait()
     put(out_ref, 1, runs, dot(rd_ref[...], g_ref[...], 1, 1))
-    second = ship(1, out_ref, out_hbm, sems)
-    second.start()
-    first.wait()
-    second.wait()
 
 
 def middle_kernel(came, runs, recv_ref, ru_ref, ld_ref, out_hbm, hid_ref, pre_ref, out_ref, sems):
@@ -116,7 +107,7 @@
     back_ref[...] = dot(take(recv_ref, 1, came), lu_ref[...], 0, 1).astype(BF16)
 
 
-def call(kernel, outs, flops, *args, scratch=(), vmem=PART_VMEM, **specs):
+def call(kernel, outs, flops, *args, scratch=(), **specs):
     moved = sum(a.size * 2 for a in args) + sum(math.prod(o) * 2 for o in outs)
     single = len(outs) == 1
     shapes = [jax.ShapeDtypeStruct(o, BF16) for o in outs]
@@ -124,7 +115,7 @@
         kernel,
         out_shape=shapes[0] if single else shapes,
         scratch_shapes=list(scratch),
-        compiler_params=pltpu.CompilerParams(vmem_limit_bytes=vmem),
+        compiler_params=pltpu.CompilerParams(vmem_limit_bytes=48 * 1024 * 1024),
         cost_estimate=pl.CostEstimate(flops=flops, bytes_accessed=moved, transcendentals=0),
         **specs,
     )(*args)
@@ -150,15 +141,9 @@
         functools.partial(send_kernel, runs),
         [message],
         2 * unit,
-        activations,
-        cotangent,
-        lu,
-        rd,
-        vmem=WHOLE_VMEM,
-        scratch=[pltpu.VMEM(s, BF16) for s in (tall, tall, square, square, message)]
-        + [dma((4,)), dma((2,))],
+        *(pltpu.with_memory_space_constraint(a, pltpu.HBM) for a in (activations, cotangent, lu, rd)),
+        scratch=[pltpu.VMEM(s, BF16) for s in (tall, tall, square, square)] + [dma((4,))],
         in_specs=[IN_HBM] * 4,
-        out_specs=IN_HBM,
     )
     first = exchange(sent, order)
     sent, hidden, pre_back = call(
@@ -199,9 +184,14 @@
 
 
 def group_order():
-    members = np.arange(math.prod(MP_AXES)).reshape(MP_AXES)
-    far = [extent // 2 for extent in MP_AXES[:3]]
-    return tuple(int(m) for m in np.roll(members, [-f for f in far], (0, 1, 2)).reshape(-1))
+    coords = [np.unravel_index(m, MP_AXES) for m in range(math.prod(MP_AXES))]
+    far = int(np.ravel_multi_index([extent // 2 for extent in MP_AXES], MP_AXES))
+
+    def hops(member):
+        y, x, z, core = (int(c) for c in coords[member])
+        return (min(y, MP_AXES[0] - y) + x + min(z, MP_AXES[2] - z), core)
+
+    return (far, *sorted((m for m in range(len(coords)) if m != far), key=hops))
 
 
 def solution(mesh):

time: 65.4 us -> 63.3 us (0.968)
  starting transfers between devices: 18.5 us -> 17.6 us
  Pallas kernels: 5.88 us -> 5.11 us
    all_to_all x1, starting transfers between devices: 13.4 us -> 12 us  [exchange(): lax.all_to_all(pieces, 'mp', split_axis=0, concat_axis=0, tiled=True, axi...]
    ppermute x1, waiting for transfers between devices: 3.55 us -> 4.32 us  [body(): mid_other = lax.ppermute(mid, 'dp', pair)]
    pallas_call x5, Pallas kernels: 5.88 us -> 5.11 us  [call(): pl.pallas_call(kernel, out_shape=shapes[0] if single else shapes, scratch...]
where the time goes in v3:
time: 63.3 us; the launch traced here: 63 us
  blocking collectives  29 us (46%)
  starting transfers between devices  17.6 us (28%)
  waiting for transfers between devices  9.2 us (15%)
  Pallas kernels  5.11 us (8%)
  local copies, waits for them, and re-layouts  1.35 us (2%)
  between operations  0.73 us (1%)
    all_to_all x1, blocking collectives, exchange(): lax.all_to_all(pieces, 'mp', split_axis=0, concat_axis=0, tiled=True, axi...  29 us
    all_to_all x1, starting transfers between devices, exchange(): lax.all_to_all(pieces, 'mp', split_axis=0, concat_axis=0, tiled=True, axi...  12 us
    pallas_call x5, Pallas kernels, call(): pl.pallas_call(kernel, out_shape=shapes[0] if single else shapes, scratch...  5.11 us
    all_to_all x1, waiting for transfers between devices, exchange(): lax.all_to_all(pieces, 'mp', split_axis=0, concat_axis=0, tiled=True, axi...  4.79 us
    ppermute x1, waiting for transfers between devices, body(): mid_other = lax.ppermute(mid, 'dp', pair)  4.32 us
    ppermute x1, starting transfers between devices, body(): last_other = lax.ppermute(last, 'dp', pair)  2.8 us
    ppermute x1, starting transfers between devices, body(): mid_other = lax.ppermute(mid, 'dp', pair)  2.8 us
  transfers between devices with their start and end apart: 3, of which 3 were waited for; matrix products, arithmetic and copies ran while one was open for 1% of the time, Pallas kernels for 2%

profile of v3, /device:TPU:1, one launch (start us, length us, event | category | flops | bytes accessed | tf_op | source)
XLA Modules:
  0.0 63.0 jit_solution(1102543871121883638)
XLA Ops:
  0.6 1.6 %shard_map.109 = bf16[128,16,128]{2,1,0:T(8,128)(2,1)S(1)} custom-call(bf16[1024,128]{1,0:T(8,128)(2,1)} %x_ref.1, bf16[1024,128]{1,0:T(8,128)(2,1)} %g_ref.1, bf16[128,128]{1,0:T(8,128)(2,1)} %bitcast.4, bf16[128,128]{1,0:T(8,128)(2,1)} %bitcast.6), custom_call_target="tpu_custom_call" | custom-call | flops 67108864 | bytes 1114112 | tf_op jit(solution)/shard_map/pallas_call | solution.py:114
  2.2 0.0 copy-start.4
  2.2 0.0 copy-start.5
  2.2 29.0 %all_to_all.10.recv_ref = bf16[128,16,128]{2,1,0:T(8,128)(2,1)S(1)} all-to-all(bf16[128,16,128]{2,1,0:T(8,128)(2,1)S(1)} %shard_map.109), channel_id=1, replica_groups={{89,0,1,2,14,16,32,96,3,15,17,33,97,4,12,18,30,34,46,48,64,98,110,112,5..., dimensions={0} | all-to-all | bytes 1048576 | tf_op jit(solution)/shard_map/all_to_all | solution.py:125
  31.2 0.0 copy-done.4
  31.2 0.0 copy-done.5
  31.2 1.7 %shard_map.110 = (bf16[128,16,128]{2,1,0:T(8,128)(2,1)}, bf16[128,1024]{1,0:T(8,128)(2,1)S(1)}, bf16[128,1024]{1,0:T(8,128)(2,1)S(1)}) custom-call(bf16[128,16,128]{2,1,0:T(8,128)(2,1)S(1)} %all_to_all.10.recv_ref, bf16[128,128]{1,0:T(8,128)(2,1)S(1)} %bitcast.8, bf16[128,128]{1,0:T(8,128)(2,1)S(1)} %bitcast.9), custom_call_target="tpu_custom_call" | custom-call | flops 134217728 | bytes 1638400 | tf_op jit(solution)/shard_map/pallas_call | solution.py:114
  32.9 12.0 %all-to-all-start.1 = ((bf16[128,16,128]{2,1,0:T(8,128)(2,1)}), bf16[128,16,128]{2,1,0:T(8,128)(2,1)S(1)}, u32[]{:S(2)}, u32[]{:S(2)}) async-start(bf16[128,16,128]{2,1,0:T(8,128)(2,1)} %get-tuple-element.11), calls=%async_computation.1 | async-start | bytes 1048576 | tf_op jit(solution)/shard_map/all_to_all | solution.py:125
  44.9 0.0 copy-start.1
  44.9 0.3 shard_map.113
  45.3 0.0 copy-start
  45.3 2.8 %collective-permute-start.1 = (bf16[2,128,128]{2,1,0:T(8,128)(2,1)S(1)}, bf16[2,128,128]{2,1,0:T(8,128)(2,1)S(1)}, u32[]{:S(2)}, u32[]{:S(2)}) collective-permute-start(bf16[2,128,128]{2,1,0:T(8,128)(2,1)S(1)} %shard_map.113), channel_id=1, source_target_pairs={{0,128},{128,0},{1,129},{129,1},{2,130},{130,2},{3,131},{131,3},{4... | collective-permute-start | bytes 196616 | tf_op jit(solution)/shard_map/ppermute | solution.py:168
  48.1 4.3 %collective-permute-done.1 = bf16[2,128,128]{2,1,0:T(8,128)(2,1)S(1)} collective-permute-done((bf16[2,128,128]{2,1,0:T(8,128)(2,1)S(1)}, bf16[2,128,128]{2,1,0:T(8,128)(2,1)S(1)}, u32[]{:S(2)}, u32[]{:S(2)}) %collective-permute-start.1) | collective-permute-done | bytes 65568 | tf_op jit(solution)/shard_map/ppermute | solution.py:168
  52.4 4.8 %all-to-all-done.1.recv_ref = bf16[128,16,128]{2,1,0:T(8,128)(2,1)S(1)} async-done(((bf16[128,16,128]{2,1,0:T(8,128)(2,1)}), bf16[128,16,128]{2,1,0:T(8,128)(2,1)S(1)}, u32[]{:S(2)}, u32[]{:S(2)}) %all-to-all-start.1) | async-done | bytes 524320 | tf_op jit(solution)/shard_map/all_to_all | solution.py:125
  57.2 0.0 copy-done.1
  57.2 0.0 copy-done
  57.2 0.4 shard_map.112
  57.6 0.0 copy-start.2
  57.6 0.0 copy-start.3
  57.6 2.8 %collective-permute-start = (bf16[2,128,128]{2,1,0:T(8,128)(2,1)S(1)}, bf16[2,128,128]{2,1,0:T(8,128)(2,1)S(1)}, u32[]{:S(2)}, u32[]{:S(2)}) collective-permute-start(bf16[2,128,128]{2,1,0:T(8,128)(2,1)S(1)} %shard_map.112), channel_id=1, source_target_pairs={{0,128},{128,0},{1,129},{129,1},{2,130},{130,2},{3,131},{131,3},{4... | collective-permute-start | bytes 196616 | tf_op jit(solution)/shard_map/ppermute | solution.py:177
  60.4 0.7 %fusion.1 = (f32[1,128,128]{2,1,0:T(8,128)}, f32[1,128,128]{2,1,0:T(8,128)}) fusion(f32[2,128,128]{2,1,0:T(8,128)S(1)} %convert_add_fusion), kind=kLoop, calls=%fused_computation.3 | loop fusion | bytes 262144 | tf_op jit(solution)/shard_map/slice | solution.py:183
  61.1 0.0 copy-done.2
  61.1 0.0 copy-done.3
  61.1 1.2 %shard_map.111 = (bf16[1024,128]{1,0:T(8,128)(2,1)}, bf16[1024,128]{1,0:T(8,128)(2,1)}) custom-call(bf16[128,16,128]{2,1,0:T(8,128)(2,1)S(1)} %all-to-all-done.1.recv_ref, bf16[128,128]{1,0:T(8,128)(2,1)S(1)} %bitcast.5, bf16[128,128]{1,0:T(8,128)(2,1)S(1)} %bitcast.7), custom_call_target="tpu_custom_call" | custom-call | flops 67108864 | bytes 1114112 | tf_op jit(solution)/shard_map/pallas_call | solution.py:114
  62.3 0.1 collective-permute-done
  62.4 0.7 %fusion = (f32[1,128,128]{2,1,0:T(8,128)}, f32[1,128,128]{2,1,0:T(8,128)}) fusion(f32[2,128,128]{2,1,0:T(8,128)S(1)} %convert_add_fusion.1), kind=kLoop, calls=%fused_computation.2 | loop fusion | bytes 262144 | tf_op jit(solution)/shard_map/slice | solution.py:183
  (2 shorter events, 0.0 us)
Async XLA Ops:
  2.2 29.0 %copy-start.4 = (bf16[1,128,128]{2,1,0:T(8,128)(2,1)S(1)}, bf16[1,128,128]{2,1,0:T(8,128)(2,1)}, u32[]{:S(2)}) copy-start(bf16[1,128,128]{2,1,0:T(8,128)(2,1)} %param.8) | copy-start | bytes 98308
  2.2 29.0 %copy-start.5 = (bf16[1,128,128]{2,1,0:T(8,128)(2,1)S(1)}, bf16[1,128,128]{2,1,0:T(8,128)(2,1)}, u32[]{:S(2)}) copy-start(bf16[1,128,128]{2,1,0:T(8,128)(2,1)} %param.9) | copy-start | bytes 98308
  32.9 24.3 %all-to-all-start.1 = ((bf16[128,16,128]{2,1,0:T(8,128)(2,1)}), bf16[128,16,128]{2,1,0:T(8,128)(2,1)S(1)}, u32[]{:S(2)}, u32[]{:S(2)}) async-start(bf16[128,16,128]{2,1,0:T(8,128)(2,1)} %get-tuple-element.11), calls=%async_computation.1 | async-start | bytes 1048576 | tf_op jit(solution)/shard_map/all_to_all | solution.py:125
  44.9 12.3 %copy-start.1 = (bf16[1024,128]{1,0:T(8,128)(2,1)S(1)}, bf16[1024,128]{1,0:T(8,128)(2,1)}, u32[]{:S(2)}) copy-start(bf16[1024,128]{1,0:T(8,128)(2,1)} %g_ref.1) | copy-start | bytes 786436
  45.3 12.0 %copy-start = (bf16[1024,128]{1,0:T(8,128)(2,1)S(1)}, bf16[1024,128]{1,0:T(8,128)(2,1)}, u32[]{:S(2)}) copy-start(bf16[1024,128]{1,0:T(8,128)(2,1)} %x_ref.1) | copy-start | bytes 786436
  45.3 7.1 %collective-permute-start.1 = (bf16[2,128,128]{2,1,0:T(8,128)(2,1)S(1)}, bf16[2,128,128]{2,1,0:T(8,128)(2,1)S(1)}, u32[]{:S(2)}, u32[]{:S(2)}) collective-permute-start(bf16[2,128,128]{2,1,0:T(8,128)(2,1)S(1)} %shard_map.113), channel_id=1, source_target_pairs={{0,128},{128,0},{1,129},{129,1},{2,130},{130,2},{3,131},{131,3},{4... | collective-permute-start | bytes 196616 | tf_op jit(solution)/shard_map/ppermute | solution.py:168
  57.6 3.5 %copy-start.2 = (bf16[1,128,128]{2,1,0:T(8,128)(2,1)S(1)}, bf16[1,128,128]{2,1,0:T(8,128)(2,1)}, u32[]{:S(2)}) copy-start(bf16[1,128,128]{2,1,0:T(8,128)(2,1)} %param.7) | copy-start | bytes 98308
  57.6 3.5 %copy-start.3 = (bf16[1,128,128]{2,1,0:T(8,128)(2,1)S(1)}, bf16[1,128,128]{2,1,0:T(8,128)(2,1)}, u32[]{:S(2)}) copy-start(bf16[1,128,128]{2,1,0:T(8,128)(2,1)} %param.10) | copy-start | bytes 98308
  57.6 4.7 %collective-permute-start = (bf16[2,128,128]{2,1,0:T(8,128)(2,1)S(1)}, bf16[2,128,128]{2,1,0:T(8,128)(2,1)S(1)}, u32[]{:S(2)}, u32[]{:S(2)}) collective-permute-start(bf16[2,128,128]{2,1,0:T(8,128)(2,1)S(1)} %shard_map.112), channel_id=1, source_target_pairs={{0,128},{128,0},{1,129},{129,1},{2,130},{130,2},{3,131},{131,3},{4... | collective-permute-start | bytes 196616 | tf_op jit(solution)/shard_map/ppermute | solution.py:177

commit v4 on v3

--- a/solution.py
+++ b/solution.py
@@ -55,12 +55,6 @@
     return pieces.reshape(pieces.shape[0], rows * LANES)
 
 
-def ship(half, out_ref, out_hbm, sems):
-    rows = out_ref.shape[1] // 2
-    part = pl.ds(half * rows, rows)
-    return pltpu.make_async_copy(out_ref.at[:, part, :], out_hbm.at[:, part, :], sems.at[half])
-
-
 def send_kernel(runs, x_hbm, g_hbm, lu_hbm, rd_hbm, out_ref, x_ref, g_ref, lu_ref, rd_ref, sems):
     pairs = ((lu_hbm, lu_ref), (x_hbm, x_ref), (rd_hbm, rd_ref), (g_hbm, g_ref))
     copies = [pltpu.make_async_copy(a, b, sems.at[i]) for i, (a, b) in enumerate(pairs)]
@@ -74,22 +68,16 @@
     put(out_ref, 1, runs, dot(rd_ref[...], g_ref[...], 1, 1))
 
 
-def middle_kernel(came, runs, recv_ref, ru_ref, ld_ref, out_hbm, hid_ref, pre_ref, out_ref, sems):
+def middle_kernel(came, runs, recv_ref, ru_ref, ld_ref, out_ref, hid_ref, pre_ref):
     ru, ld = ru_ref[...], ld_ref[...]
     pre_act = dot(ru, take(recv_ref, 0, came), 0, 0)
     hidden = gelu_exact(pre_act).astype(BF16)
+    hid_ref[...] = hidden
     put(out_ref, 0, runs, dot(ld, hidden, 0, 0))
-    first = ship(0, out_ref, out_hbm, sems)
-    first.start()
-    hid_ref[...] = hidden
     hidden_back = dot(ld, take(recv_ref, 1, came), 1, 0)
     pre_back = (hidden_back * gelu_slope(pre_act)).astype(BF16)
     put(out_ref, 1, runs, dot(ru, pre_back, 1, 0))
-    second = ship(1, out_ref, out_hbm, sems)
-    second.start()
     pre_ref[...] = pre_back
-    first.wait()
-    second.wait()
 
 
 def middle_grads_kernel(came, recv_ref, hid_ref, pre_ref, grads_ref):
@@ -153,8 +141,6 @@
         first,
         ru,
         ld,
-        scratch=[pltpu.VMEM(message, BF16), dma((2,))],
-        out_specs=[IN_HBM, IN_VMEM, IN_VMEM],
     )
     second = exchange(sent, order)
     mid = call(
@@ -189,7 +175,7 @@
 
     def hops(member):
         y, x, z, core = (int(c) for c in coords[member])
-        return (min(y, MP_AXES[0] - y) + x + min(z, MP_AXES[2] - z), core)
+        return (-core, min(y, MP_AXES[0] - y) + x + min(z, MP_AXES[2] - z))
 
     return (far, *sorted((m for m in range(len(coords)) if m != far), key=hops))
 

time: 63.3 us -> 63.1 us (level)
    ppermute x1, waiting for transfers between devices: 4.32 us -> 3.06 us  [body(): mid_other = lax.ppermute(mid, 'dp', pair)]
    all_to_all x1, waiting for transfers between devices: 4.79 us -> 5.6 us  [exchange(): lax.all_to_all(pieces, 'mp', split_axis=0, concat_axis=0, tiled=True, axi...]
where the time goes in v4:
time: 63.1 us; the launch traced here: 62.5 us
  blocking collectives  28.5 us (45%)
  starting transfers between devices  18 us (29%)
  waiting for transfers between devices  8.73 us (14%)
  Pallas kernels  5.16 us (8%)
  local copies, waits for them, and re-layouts  1.35 us (2%)
  between operations  0.72 us (1%)
    all_to_all x1, blocking collectives, exchange(): lax.all_to_all(pieces, 'mp', split_axis=0, concat_axis=0, tiled=True, axi...  28.5 us
    all_to_all x1, starting transfers between devices, exchange(): lax.all_to_all(pieces, 'mp', split_axis=0, concat_axis=0, tiled=True, axi...  12.4 us
    all_to_all x1, waiting for transfers between devices, exchange(): lax.all_to_all(pieces, 'mp', split_axis=0, concat_axis=0, tiled=True, axi...  5.6 us
    pallas_call x5, Pallas kernels, call(): pl.pallas_call(kernel, out_shape=shapes[0] if single else shapes, scratch...  5.16 us
    ppermute x1, waiting for transfers between devices, body(): mid_other = lax.ppermute(mid, 'dp', pair)  3.06 us
    ppermute x1, starting transfers between devices, body(): last_other = lax.ppermute(last, 'dp', pair)  2.8 us
    ppermute x1, starting transfers between devices, body(): mid_other = lax.ppermute(mid, 'dp', pair)  2.8 us
  transfers between devices with their start and end apart: 3, of which 3 were waited for; matrix products, arithmetic and copies ran while one was open for 1% of the time, Pallas kernels for 2%

profile of v4, /device:TPU:1, one launch (start us, length us, event | category | flops | bytes accessed | tf_op | source)
XLA Modules:
  0.0 62.5 jit_solution(10449196211926271220)
XLA Ops:
  0.6 1.6 %shard_map.109 = bf16[128,16,128]{2,1,0:T(8,128)(2,1)S(1)} custom-call(bf16[1024,128]{1,0:T(8,128)(2,1)} %x_ref.1, bf16[1024,128]{1,0:T(8,128)(2,1)} %g_ref.1, bf16[128,128]{1,0:T(8,128)(2,1)} %bitcast.4, bf16[128,128]{1,0:T(8,128)(2,1)} %bitcast.6), custom_call_target="tpu_custom_call" | custom-call | flops 67108864 | bytes 1114112 | tf_op jit(solution)/shard_map/pallas_call | solution.py:102
  2.2 0.0 copy-start.4
  2.2 0.0 copy-start.5
  2.2 28.5 %all_to_all.10.recv_ref = bf16[128,16,128]{2,1,0:T(8,128)(2,1)S(1)} all-to-all(bf16[128,16,128]{2,1,0:T(8,128)(2,1)S(1)} %shard_map.109), channel_id=1, replica_groups={{89,1,3,15,17,33,97,5,13,19,31,35,47,49,65,99,111,113,7,11,21,29,37,45,..., dimensions={0} | all-to-all | bytes 1048576 | tf_op jit(solution)/shard_map/all_to_all | solution.py:113
  30.7 0.0 copy-done.4
  30.7 0.0 copy-done.5
  30.7 1.7 %shard_map.110 = (bf16[128,16,128]{2,1,0:T(8,128)(2,1)}, bf16[128,1024]{1,0:T(8,128)(2,1)S(1)}, bf16[128,1024]{1,0:T(8,128)(2,1)S(1)}) custom-call(bf16[128,16,128]{2,1,0:T(8,128)(2,1)S(1)} %all_to_all.10.recv_ref, bf16[128,128]{1,0:T(8,128)(2,1)S(1)} %bitcast.8, bf16[128,128]{1,0:T(8,128)(2,1)S(1)} %bitcast.9), custom_call_target="tpu_custom_call" | custom-call | flops 134217728 | bytes 1638400 | tf_op jit(solution)/shard_map/pallas_call | solution.py:102
  32.4 12.4 %all-to-all-start.1 = ((bf16[128,16,128]{2,1,0:T(8,128)(2,1)}), bf16[128,16,128]{2,1,0:T(8,128)(2,1)S(1)}, u32[]{:S(2)}, u32[]{:S(2)}) async-start(bf16[128,16,128]{2,1,0:T(8,128)(2,1)} %get-tuple-element.11), calls=%async_computation.1 | async-start | bytes 1048576 | tf_op jit(solution)/shard_map/all_to_all | solution.py:113
  44.9 0.0 copy-start.1
  44.9 0.3 shard_map.113
  45.2 0.0 copy-start
  45.2 2.8 %collective-permute-start.1 = (bf16[2,128,128]{2,1,0:T(8,128)(2,1)S(1)}, bf16[2,128,128]{2,1,0:T(8,128)(2,1)S(1)}, u32[]{:S(2)}, u32[]{:S(2)}) collective-permute-start(bf16[2,128,128]{2,1,0:T(8,128)(2,1)S(1)} %shard_map.113), channel_id=1, source_target_pairs={{0,128},{128,0},{1,129},{129,1},{2,130},{130,2},{3,131},{131,3},{4... | collective-permute-start | bytes 196616 | tf_op jit(solution)/shard_map/ppermute | solution.py:154
  48.0 3.1 %collective-permute-done.1 = bf16[2,128,128]{2,1,0:T(8,128)(2,1)S(1)} collective-permute-done((bf16[2,128,128]{2,1,0:T(8,128)(2,1)S(1)}, bf16[2,128,128]{2,1,0:T(8,128)(2,1)S(1)}, u32[]{:S(2)}, u32[]{:S(2)}) %collective-permute-start.1) | collective-permute-done | bytes 65568 | tf_op jit(solution)/shard_map/ppermute | solution.py:154
  51.1 5.6 %all-to-all-done.1.recv_ref = bf16[128,16,128]{2,1,0:T(8,128)(2,1)S(1)} async-done(((bf16[128,16,128]{2,1,0:T(8,128)(2,1)}), bf16[128,16,128]{2,1,0:T(8,128)(2,1)S(1)}, u32[]{:S(2)}, u32[]{:S(2)}) %all-to-all-start.1) | async-done | bytes 524320 | tf_op jit(solution)/shard_map/all_to_all | solution.py:113
  56.7 0.0 copy-done.1
  56.7 0.0 copy-done
  56.7 0.4 shard_map.112
  57.1 0.0 copy-start.2
  57.1 0.0 copy-start.3
  57.1 2.8 %collective-permute-start = (bf16[2,128,128]{2,1,0:T(8,128)(2,1)S(1)}, bf16[2,128,128]{2,1,0:T(8,128)(2,1)S(1)}, u32[]{:S(2)}, u32[]{:S(2)}) collective-permute-start(bf16[2,128,128]{2,1,0:T(8,128)(2,1)S(1)} %shard_map.112), channel_id=1, source_target_pairs={{0,128},{128,0},{1,129},{129,1},{2,130},{130,2},{3,131},{131,3},{4... | collective-permute-start | bytes 196616 | tf_op jit(solution)/shard_map/ppermute | solution.py:163
  59.9 0.7 %fusion.1 = (f32[1,128,128]{2,1,0:T(8,128)}, f32[1,128,128]{2,1,0:T(8,128)}) fusion(f32[2,128,128]{2,1,0:T(8,128)S(1)} %convert_add_fusion), kind=kLoop, calls=%fused_computation.3 | loop fusion | bytes 262144 | tf_op jit(solution)/shard_map/slice | solution.py:169
  60.6 0.0 copy-done.2
  60.6 0.0 copy-done.3
  60.6 1.2 %shard_map.111 = (bf16[1024,128]{1,0:T(8,128)(2,1)}, bf16[1024,128]{1,0:T(8,128)(2,1)}) custom-call(bf16[128,16,128]{2,1,0:T(8,128)(2,1)S(1)} %all-to-all-done.1.recv_ref, bf16[128,128]{1,0:T(8,128)(2,1)S(1)} %bitcast.5, bf16[128,128]{1,0:T(8,128)(2,1)S(1)} %bitcast.7), custom_call_target="tpu_custom_call" | custom-call | flops 67108864 | bytes 1114112 | tf_op jit(solution)/shard_map/pallas_call | solution.py:102
  61.8 0.1 collective-permute-done
  61.8 0.7 %fusion = (f32[1,128,128]{2,1,0:T(8,128)}, f32[1,128,128]{2,1,0:T(8,128)}) fusion(f32[2,128,128]{2,1,0:T(8,128)S(1)} %convert_add_fusion.1), kind=kLoop, calls=%fused_computation.2 | loop fusion | bytes 262144 | tf_op jit(solution)/shard_map/slice | solution.py:169
  (2 shorter events, 0.0 us)
Async XLA Ops:
  2.2 28.5 %copy-start.4 = (bf16[1,128,128]{2,1,0:T(8,128)(2,1)S(1)}, bf16[1,128,128]{2,1,0:T(8,128)(2,1)}, u32[]{:S(2)}) copy-start(bf16[1,128,128]{2,1,0:T(8,128)(2,1)} %param.8) | copy-start | bytes 98308
  2.2 28.5 %copy-start.5 = (bf16[1,128,128]{2,1,0:T(8,128)(2,1)S(1)}, bf16[1,128,128]{2,1,0:T(8,128)(2,1)}, u32[]{:S(2)}) copy-start(bf16[1,128,128]{2,1,0:T(8,128)(2,1)} %param.9) | copy-start | bytes 98308
  32.4 24.3 %all-to-all-start.1 = ((bf16[128,16,128]{2,1,0:T(8,128)(2,1)}), bf16[128,16,128]{2,1,0:T(8,128)(2,1)S(1)}, u32[]{:S(2)}, u32[]{:S(2)}) async-start(bf16[128,16,128]{2,1,0:T(8,128)(2,1)} %get-tuple-element.11), calls=%async_computation.1 | async-start | bytes 1048576 | tf_op jit(solution)/shard_map/all_to_all | solution.py:113
  44.9 11.8 %copy-start.1 = (bf16[1024,128]{1,0:T(8,128)(2,1)S(1)}, bf16[1024,128]{1,0:T(8,128)(2,1)}, u32[]{:S(2)}) copy-start(bf16[1024,128]{1,0:T(8,128)(2,1)} %g_ref.1) | copy-start | bytes 786436
  45.2 11.5 %copy-start = (bf16[1024,128]{1,0:T(8,128)(2,1)S(1)}, bf16[1024,128]{1,0:T(8,128)(2,1)}, u32[]{:S(2)}) copy-start(bf16[1024,128]{1,0:T(8,128)(2,1)} %x_ref.1) | copy-start | bytes 786436
  45.2 5.9 %collective-permute-start.1 = (bf16[2,128,128]{2,1,0:T(8,128)(2,1)S(1)}, bf16[2,128,128]{2,1,0:T(8,128)(2,1)S(1)}, u32[]{:S(2)}, u32[]{:S(2)}) collective-permute-start(bf16[2,128,128]{2,1,0:T(8,128)(2,1)S(1)} %shard_map.113), channel_id=1, source_target_pairs={{0,128},{128,0},{1,129},{129,1},{2,130},{130,2},{3,131},{131,3},{4... | collective-permute-start | bytes 196616 | tf_op jit(solution)/shard_map/ppermute | solution.py:154
  57.1 3.5 %copy-start.2 = (bf16[1,128,128]{2,1,0:T(8,128)(2,1)S(1)}, bf16[1,128,128]{2,1,0:T(8,128)(2,1)}, u32[]{:S(2)}) copy-start(bf16[1,128,128]{2,1,0:T(8,128)(2,1)} %param.7) | copy-start | bytes 98308
  57.1 3.5 %copy-start.3 = (bf16[1,128,128]{2,1,0:T(8,128)(2,1)S(1)}, bf16[1,128,128]{2,1,0:T(8,128)(2,1)}, u32[]{:S(2)}) copy-start(bf16[1,128,128]{2,1,0:T(8,128)(2,1)} %param.10) | copy-start | bytes 98308
  57.1 4.7 %collective-permute-start = (bf16[2,128,128]{2,1,0:T(8,128)(2,1)S(1)}, bf16[2,128,128]{2,1,0:T(8,128)(2,1)S(1)}, u32[]{:S(2)}, u32[]{:S(2)}) collective-permute-start(bf16[2,128,128]{2,1,0:T(8,128)(2,1)S(1)} %shard_map.112), channel_id=1, source_target_pairs={{0,128},{128,0},{1,129},{129,1},{2,130},{130,2},{3,131},{131,3},{4... | collective-permute-start | bytes 196616 | tf_op jit(solution)/shard_map/ppermute | solution.py:163

commit v5 on v4

--- a/solution.py
+++ b/solution.py
@@ -17,14 +17,10 @@
 IN_VMEM = pl.BlockSpec(memory_space=pltpu.VMEM)
 
 
-def gelu_exact(value):
-    return 0.5 * value * (1.0 + lax.erf(value / math.sqrt(2.0)))
-
-
-def gelu_slope(value):
+def gelu_and_slope(value):
     cumul = 0.5 * (1.0 + lax.erf(value / math.sqrt(2.0)))
     density = jnp.exp(-0.5 * value * value) / math.sqrt(2.0 * math.pi)
-    return cumul + value * density
+    return value * cumul, cumul + value * density
 
 
 def dot(a, b, ca, cb):
@@ -71,11 +67,12 @@
 def middle_kernel(came, runs, recv_ref, ru_ref, ld_ref, out_ref, hid_ref, pre_ref):
     ru, ld = ru_ref[...], ld_ref[...]
     pre_act = dot(ru, take(recv_ref, 0, came), 0, 0)
-    hidden = gelu_exact(pre_act).astype(BF16)
+    hidden, slope = gelu_and_slope(pre_act)
+    hidden = hidden.astype(BF16)
     hid_ref[...] = hidden
     put(out_ref, 0, runs, dot(ld, hidden, 0, 0))
     hidden_back = dot(ld, take(recv_ref, 1, came), 1, 0)
-    pre_back = (hidden_back * gelu_slope(pre_act)).astype(BF16)
+    pre_back = (hidden_back * slope).astype(BF16)
     put(out_ref, 1, runs, dot(ru, pre_back, 1, 0))
     pre_ref[...] = pre_back
 
@@ -175,7 +172,8 @@
 
     def hops(member):
         y, x, z, core = (int(c) for c in coords[member])
-        return (-core, min(y, MP_AXES[0] - y) + x + min(z, MP_AXES[2] - z))
+        up = min(y, MP_AXES[0] - y)
+        return (-core, up, up + x + min(z, MP_AXES[2] - z))
 
     return (far, *sorted((m for m in range(len(coords)) if m != far), key=hops))
 

time: 63.1 us -> 62.9 us (level)
  no operation moved by 1% of the time
where the time goes in v5:
time: 62.9 us; the launch traced here: 62.6 us
  blocking collectives  28.7 us (46%)
  starting transfers between devices  17.7 us (28%)
  waiting for transfers between devices  8.95 us (14%)
  Pallas kernels  5.14 us (8%)
  local copies, waits for them, and re-layouts  1.35 us (2%)
  between operations  0.72 us (1%)
    all_to_all x1, blocking collectives, exchange(): lax.all_to_all(pieces, 'mp', split_axis=0, concat_axis=0, tiled=True, axi...  28.7 us
    all_to_all x1, starting transfers between devices, exchange(): lax.all_to_all(pieces, 'mp', split_axis=0, concat_axis=0, tiled=True, axi...  12.1 us
    all_to_all x1, waiting for transfers between devices, exchange(): lax.all_to_all(pieces, 'mp', split_axis=0, concat_axis=0, tiled=True, axi...  5.35 us
    pallas_call x5, Pallas kernels, call(): pl.pallas_call(kernel, out_shape=shapes[0] if single else shapes, scratch...  5.14 us
    ppermute x1, waiting for transfers between devices, body(): mid_other = lax.ppermute(mid, 'dp', pair)  3.53 us
    ppermute x1, starting transfers between devices, body(): mid_other = lax.ppermute(mid, 'dp', pair)  2.8 us
    ppermute x1, starting transfers between devices, body(): last_other = lax.ppermute(last, 'dp', pair)  2.8 us
  transfers between devices with their start and end apart: 3, of which 3 were waited for; matrix products, arithmetic and copies ran while one was open for 1% of the time, Pallas kernels for 2%

profile of v5, /device:TPU:1, one launch (start us, length us, event | category | flops | bytes accessed | tf_op | source)
XLA Modules:
  0.0 62.6 jit_solution(6262908208190274224)
XLA Ops:
  0.6 1.6 %shard_map.109 = bf16[128,16,128]{2,1,0:T(8,128)(2,1)S(1)} custom-call(bf16[1024,128]{1,0:T(8,128)(2,1)} %x_ref.1, bf16[1024,128]{1,0:T(8,128)(2,1)} %g_ref.1, bf16[128,128]{1,0:T(8,128)(2,1)} %bitcast.4, bf16[128,128]{1,0:T(8,128)(2,1)} %bitcast.6), custom_call_target="tpu_custom_call" | custom-call | flops 67108864 | bytes 1114112 | tf_op jit(solution)/shard_map/pallas_call | solution.py:99
  2.2 0.0 copy-start.4
  2.2 0.0 copy-start.5
  2.2 28.7 %all_to_all.10.recv_ref = bf16[128,16,128]{2,1,0:T(8,128)(2,1)S(1)} all-to-all(bf16[128,16,128]{2,1,0:T(8,128)(2,1)S(1)} %shard_map.109), channel_id=1, replica_groups={{89,1,3,15,17,5,13,19,31,7,11,21,29,9,23,27,25,33,97,35,47,49,99,111,11..., dimensions={0} | all-to-all | bytes 1048576 | tf_op jit(solution)/shard_map/all_to_all | solution.py:110
  30.9 0.0 copy-done.4
  30.9 0.0 copy-done.5
  30.9 1.7 %shard_map.110 = (bf16[128,16,128]{2,1,0:T(8,128)(2,1)}, bf16[128,1024]{1,0:T(8,128)(2,1)S(1)}, bf16[128,1024]{1,0:T(8,128)(2,1)S(1)}) custom-call(bf16[128,16,128]{2,1,0:T(8,128)(2,1)S(1)} %all_to_all.10.recv_ref, bf16[128,128]{1,0:T(8,128)(2,1)S(1)} %bitcast.8, bf16[128,128]{1,0:T(8,128)(2,1)S(1)} %bitcast.9), custom_call_target="tpu_custom_call" | custom-call | flops 134217728 | bytes 1638400 | tf_op jit(solution)/shard_map/pallas_call | solution.py:99
  32.6 12.1 %all-to-all-start.1 = ((bf16[128,16,128]{2,1,0:T(8,128)(2,1)}), bf16[128,16,128]{2,1,0:T(8,128)(2,1)S(1)}, u32[]{:S(2)}, u32[]{:S(2)}) async-start(bf16[128,16,128]{2,1,0:T(8,128)(2,1)} %get-tuple-element.11), calls=%async_computation.1 | async-start | bytes 1048576 | tf_op jit(solution)/shard_map/all_to_all | solution.py:110
  44.7 0.0 copy-start.1
  44.7 0.3 shard_map.113
  45.1 0.0 copy-start
  45.1 2.8 %collective-permute-start.1 = (bf16[2,128,128]{2,1,0:T(8,128)(2,1)S(1)}, bf16[2,128,128]{2,1,0:T(8,128)(2,1)S(1)}, u32[]{:S(2)}, u32[]{:S(2)}) collective-permute-start(bf16[2,128,128]{2,1,0:T(8,128)(2,1)S(1)} %shard_map.113), channel_id=1, source_target_pairs={{0,128},{128,0},{1,129},{129,1},{2,130},{130,2},{3,131},{131,3},{4... | collective-permute-start | bytes 196616 | tf_op jit(solution)/shard_map/ppermute | solution.py:151
  47.9 3.5 %collective-permute-done.1 = bf16[2,128,128]{2,1,0:T(8,128)(2,1)S(1)} collective-permute-done((bf16[2,128,128]{2,1,0:T(8,128)(2,1)S(1)}, bf16[2,128,128]{2,1,0:T(8,128)(2,1)S(1)}, u32[]{:S(2)}, u32[]{:S(2)}) %collective-permute-start.1) | collective-permute-done | bytes 65568 | tf_op jit(solution)/shard_map/ppermute | solution.py:151
  51.4 5.3 %all-to-all-done.1.recv_ref = bf16[128,16,128]{2,1,0:T(8,128)(2,1)S(1)} async-done(((bf16[128,16,128]{2,1,0:T(8,128)(2,1)}), bf16[128,16,128]{2,1,0:T(8,128)(2,1)S(1)}, u32[]{:S(2)}, u32[]{:S(2)}) %all-to-all-start.1) | async-done | bytes 524320 | tf_op jit(solution)/shard_map/all_to_all | solution.py:110
  56.8 0.0 copy-done.1
  56.8 0.0 copy-done
  56.8 0.4 shard_map.112
  57.2 0.0 copy-start.2
  57.2 0.0 copy-start.3
  57.2 2.8 %collective-permute-start = (bf16[2,128,128]{2,1,0:T(8,128)(2,1)S(1)}, bf16[2,128,128]{2,1,0:T(8,128)(2,1)S(1)}, u32[]{:S(2)}, u32[]{:S(2)}) collective-permute-start(bf16[2,128,128]{2,1,0:T(8,128)(2,1)S(1)} %shard_map.112), channel_id=1, source_target_pairs={{0,128},{128,0},{1,129},{129,1},{2,130},{130,2},{3,131},{131,3},{4... | collective-permute-start | bytes 196616 | tf_op jit(solution)/shard_map/ppermute | solution.py:160
  60.0 0.7 %fusion.1 = (f32[1,128,128]{2,1,0:T(8,128)}, f32[1,128,128]{2,1,0:T(8,128)}) fusion(f32[2,128,128]{2,1,0:T(8,128)S(1)} %convert_add_fusion), kind=kLoop, calls=%fused_computation.3 | loop fusion | bytes 262144 | tf_op jit(solution)/shard_map/slice | solution.py:166
  60.6 0.0 copy-done.2
  60.7 0.0 copy-done.3
  60.7 1.2 %shard_map.111 = (bf16[1024,128]{1,0:T(8,128)(2,1)}, bf16[1024,128]{1,0:T(8,128)(2,1)}) custom-call(bf16[128,16,128]{2,1,0:T(8,128)(2,1)S(1)} %all-to-all-done.1.recv_ref, bf16[128,128]{1,0:T(8,128)(2,1)S(1)} %bitcast.5, bf16[128,128]{1,0:T(8,128)(2,1)S(1)} %bitcast.7), custom_call_target="tpu_custom_call" | custom-call | flops 67108864 | bytes 1114112 | tf_op jit(solution)/shard_map/pallas_call | solution.py:99
  61.8 0.1 collective-permute-done
  61.9 0.7 %fusion = (f32[1,128,128]{2,1,0:T(8,128)}, f32[1,128,128]{2,1,0:T(8,128)}) fusion(f32[2,128,128]{2,1,0:T(8,128)S(1)} %convert_add_fusion.1), kind=kLoop, calls=%fused_computation.2 | loop fusion | bytes 262144 | tf_op jit(solution)/shard_map/slice | solution.py:166
  (2 shorter events, 0.0 us)
Async XLA Ops:
  2.2 28.7 %copy-start.4 = (bf16[1,128,128]{2,1,0:T(8,128)(2,1)S(1)}, bf16[1,128,128]{2,1,0:T(8,128)(2,1)}, u32[]{:S(2)}) copy-start(bf16[1,128,128]{2,1,0:T(8,128)(2,1)} %param.8) | copy-start | bytes 98308
  2.2 28.7 %copy-start.5 = (bf16[1,128,128]{2,1,0:T(8,128)(2,1)S(1)}, bf16[1,128,128]{2,1,0:T(8,128)(2,1)}, u32[]{:S(2)}) copy-start(bf16[1,128,128]{2,1,0:T(8,128)(2,1)} %param.9) | copy-start | bytes 98308
  32.6 24.2 %all-to-all-start.1 = ((bf16[128,16,128]{2,1,0:T(8,128)(2,1)}), bf16[128,16,128]{2,1,0:T(8,128)(2,1)S(1)}, u32[]{:S(2)}, u32[]{:S(2)}) async-start(bf16[128,16,128]{2,1,0:T(8,128)(2,1)} %get-tuple-element.11), calls=%async_computation.1 | async-start | bytes 1048576 | tf_op jit(solution)/shard_map/all_to_all | solution.py:110
  44.7 12.1 %copy-start.1 = (bf16[1024,128]{1,0:T(8,128)(2,1)S(1)}, bf16[1024,128]{1,0:T(8,128)(2,1)}, u32[]{:S(2)}) copy-start(bf16[1024,128]{1,0:T(8,128)(2,1)} %g_ref.1) | copy-start | bytes 786436
  45.1 11.7 %copy-start = (bf16[1024,128]{1,0:T(8,128)(2,1)S(1)}, bf16[1024,128]{1,0:T(8,128)(2,1)}, u32[]{:S(2)}) copy-start(bf16[1024,128]{1,0:T(8,128)(2,1)} %x_ref.1) | copy-start | bytes 786436
  45.1 6.3 %collective-permute-start.1 = (bf16[2,128,128]{2,1,0:T(8,128)(2,1)S(1)}, bf16[2,128,128]{2,1,0:T(8,128)(2,1)S(1)}, u32[]{:S(2)}, u32[]{:S(2)}) collective-permute-start(bf16[2,128,128]{2,1,0:T(8,128)(2,1)S(1)} %shard_map.113), channel_id=1, source_target_pairs={{0,128},{128,0},{1,129},{129,1},{2,130},{130,2},{3,131},{131,3},{4... | collective-permute-start | bytes 196616 | tf_op jit(solution)/shard_map/ppermute | solution.py:151
  57.2 3.5 %copy-start.2 = (bf16[1,128,128]{2,1,0:T(8,128)(2,1)S(1)}, bf16[1,128,128]{2,1,0:T(8,128)(2,1)}, u32[]{:S(2)}) copy-start(bf16[1,128,128]{2,1,0:T(8,128)(2,1)} %param.7) | copy-start | bytes 98308
  57.2 3.5 %copy-start.3 = (bf16[1,128,128]{2,1,0:T(8,128)(2,1)S(1)}, bf16[1,128,128]{2,1,0:T(8,128)(2,1)}, u32[]{:S(2)}) copy-start(bf16[1,128,128]{2,1,0:T(8,128)(2,1)} %param.10) | copy-start | bytes 98308
  57.2 4.7 %collective-permute-start = (bf16[2,128,128]{2,1,0:T(8,128)(2,1)S(1)}, bf16[2,128,128]{2,1,0:T(8,128)(2,1)S(1)}, u32[]{:S(2)}, u32[]{:S(2)}) collective-permute-start(bf16[2,128,128]{2,1,0:T(8,128)(2,1)S(1)} %shard_map.112), channel_id=1, source_target_pairs={{0,128},{128,0},{1,129},{129,1},{2,130},{130,2},{3,131},{131,3},{4... | collective-permute-start | bytes 196616 | tf_op jit(solution)/shard_map/ppermute | solution.py:160
